TPU v7x, 768 devices: a whole 4x8x12 slice. The times are simulated.
768 devices in a mesh: section: 12 (over z), dp: 4 (over y_hi), tensor: 16 (over y_lo, x, core).
Axes of the slice: x: 4, y: 8 (y_hi: 4, y_lo: 2; y = y_hi * 2 + y_lo), z: 12, core: 2. Of those that a mesh axis runs over, the one named last changes fastest.
Arguments:
- context: bfloat16 [12, 2048, 8192], P('section', 'dp', 'tensor'), may hold values from -6 to 6
- residual: bfloat16 [12, 2048, 8192], P('section', 'tensor', 'dp')
- out_weight: bfloat16 [12, 8192, 8192], P('section', 'tensor', 'dp'), may hold values from -0.0625 to 0.0625
- norm_gain: float32 [12, 8192], P('section'), may hold values from 0.25 to 1.75
- valid_tokens: int32 [12], P('section'), may hold values from 1024 to 2048, as said below
Outputs:
- normed: bfloat16 [12, 2048, 8192], P('section', 'tensor', 'dp')
- handoff: bfloat16 [12, 2048, 8192], P('section', 'tensor', 'dp')
Inputs may be any that keep to these rules, and one draw needn't show every extreme that they name: `valid_tokens`: some section's micro-batch is full in every draw.
All inputs are finite; a program needn't handle non-finite values.
Results may differ from a plain program's by a relative error of at most 0.018.
Values may be sent and summed in bfloat16 or wider, within the bound.
No kernel may reach another device: no remote copies, remote signals or barrier semaphores. Data moves between devices by JAX's collectives and lax.ppermute only.
A program may use at most 64 MiB of HBM per device.

v0:
```python
import jax
import jax.numpy as jnp
from jax import lax
from jax.sharding import PartitionSpec as P


def passed_along(value, axis, steps):
    count = lax.axis_size(axis)
    leading, last = (max(0, -steps), min(count, count - steps))
    return lax.ppermute(value, axis, [(source, source + steps) for source in range(leading, last)])


def on_device(context, residual, out_weight, norm_gain, valid_tokens):
    whole = lax.all_gather(context[0], "dp", axis=0, tiled=True)
    weight = out_weight[0]
    rows_here = residual.shape[1]
    tensor_pos = lax.axis_index("tensor")
    attn = lax.psum_scatter(
        jnp.dot(whole, weight, preferred_element_type=jnp.float32).astype(jnp.bfloat16),
        "tensor",
        scatter_dimension=0,
        tiled=True,
    ).astype(jnp.float32)
    hidden = residual[0].astype(jnp.float32) + attn
    full_rows = lax.all_to_all(
        hidden.astype(jnp.bfloat16), "dp", split_axis=0, concat_axis=1, tiled=True
    ).astype(hidden.dtype)
    mean_sq = jnp.mean(full_rows * full_rows, axis=1, keepdims=True)
    scaled = (full_rows * lax.rsqrt(mean_sq + 1e-06) * norm_gain[0][None, :]).astype(jnp.bfloat16)
    normed = lax.all_to_all(scaled, "dp", split_axis=1, concat_axis=0, tiled=True)
    row_ids = tensor_pos * rows_here + jnp.arange(rows_here, dtype=jnp.int32)
    keep = (row_ids < valid_tokens[0])[:, None]
    normed = jnp.where(keep, normed, jnp.zeros_like(normed))
    outgoing = jnp.where(keep, hidden, 0.0).astype(jnp.bfloat16)
    handoff = passed_along(outgoing, "section", 1)
    return (normed[None], handoff[None])


def solution(mesh):
    placed = (
        P("section", "dp", "tensor"),
        P("section", "tensor", "dp"),
        P("section", "tensor", "dp"),
        P("section", None),
        P("section"),
    )
    return jax.shard_map(
        on_device,
        mesh=mesh,
        in_specs=placed,
        out_specs=(P("section", "tensor", "dp"), P("section", "tensor", "dp")),
        check_vma=False,
    )
```

profile of v0, /device:TPU:71, one launch (start us, length us, event | category | flops | bytes accessed | tf_op | source)
XLA Modules:
  0.0 215.5 jit_solution(15731919373888391226)
XLA Ops:
  7.2 0.0 copy-start
  7.2 0.0 all-gather.3.cloned.1.call-start
  7.2 0.7 all-gather.3.cloned.1.call-update
  7.9 0.0 reduce-scatter.2.cloned.1.call-start
  8.0 60.9 %all-gather.3.cloned.1.call-done = bf16[1,2048,512]{2,1,0:T(8,128)(2,1)} async-done(((bf16[1,512,512]{2,1,0:T(8,128)(2,1)}), bf16[1,2048,512]{2,1,0:T(8,128)(2,1)}) %all-gather.3.cloned.1.call-update) | async-done | bytes 2097168 | tf_op jit(solution)/shard_map/all_gather | solution.py:14
  68.9 0.0 copy-done
  68.9 8.4 %convolution_convert_fusion = bf16[2048,2048]{1,0:T(8,128)(2,1)} fusion(bf16[1,512,2048]{2,1,0:T(8,128)(2,1)S(1)} %copy-done, bf16[1,2048,512]{2,1,0:T(8,128)(2,1)} %all-gather.3.cloned.1.call-done), kind=kOutput, calls=%fused_computation | convolution fusion | flops 4299161600 | bytes 12582912 | tf_op jit(solution)/shard_map/dot_general | solution.py:19
  77.3 0.0 copy-start.1
  77.3 0.0 reduce-scatter.2.cloned.1.call-update
  77.3 0.0 copy-start.3
  78.0 83.1 %reduce-scatter.2.cloned.1.call-done = bf16[128,2048]{1,0:T(8,128)(2,1)} async-done(((bf16[2048,2048]{1,0:T(8,128)(2,1)}), bf16[128,2048]{1,0:T(8,128)(2,1)}) %reduce-scatter.2.cloned.1.call-update) | async-done | bytes 524304 | tf_op jit(solution)/shard_map/reduce_scatter | solution.py:18
  161.2 0.0 copy-done.1
  161.2 2.0 select_convert_fusion
  163.2 5.8 %all-to-all-start = ((bf16[4,32,2048]{2,1,0:T(8,128)(2,1)}), bf16[4,32,2048]{2,1,0:T(8,128)(2,1)S(1)}, u32[]{:S(2)}, u32[]{:S(2)}) async-start(bf16[4,32,2048]{2,1,0:T(8,128)(2,1)} %bitcast.4), calls=%async_computation.1 | async-start | bytes 1048576 | tf_op jit(solution)/shard_map/all_to_all | solution.py:25
  169.0 0.5 broadcast.52
  169.5 0.0 copy-done.3
  169.6 0.7 reduce.5
  170.3 13.2 %all-to-all-done = bf16[4,32,2048]{2,1,0:T(8,128)(2,1)S(1)} async-done(((bf16[4,32,2048]{2,1,0:T(8,128)(2,1)}), bf16[4,32,2048]{2,1,0:T(8,128)(2,1)S(1)}, u32[]{:S(2)}, u32[]{:S(2)}) %all-to-all-start) | async-done | bytes 524320 | tf_op jit(solution)/shard_map/all_to_all | solution.py:25
  183.5 0.2 fusion.2
  183.7 1.0 fusion.6
  184.7 4.2 %all-to-all-start.1 = ((bf16[32,4,2048]{2,0,1:T(8,128)(2,1)}), bf16[32,4,2048]{2,0,1:T(8,128)(2,1)S(1)}, u32[]{:S(2)}, u32[]{:S(2)}) async-start(bf16[32,4,2048]{2,0,1:T(8,128)(2,1)} %fusion.6), calls=%async_computation.2 | async-start | bytes 1048576 | tf_op jit(solution)/shard_map/all_to_all | solution.py:30
  188.9 4.4 %collective-permute-start = (bf16[128,2048]{1,0:T(8,128)(2,1)S(1)}, bf16[128,2048]{1,0:T(8,128)(2,1)S(1)}, u32[]{:S(2)}, u32[]{:S(2)}) collective-permute-start(bf16[128,2048]{1,0:T(8,128)(2,1)S(1)} %get-tuple-element.2), channel_id=1, source_target_pairs={{0,64},{64,128},{128,192},{192,256},{256,320},{320,384},{384,448},... | collective-permute-start | bytes 1572872 | tf_op jit(solution)/shard_map/ppermute | solution.py:10
  193.3 11.7 %collective-permute-done = bf16[128,2048]{1,0:T(8,128)(2,1)S(1)} collective-permute-done((bf16[128,2048]{1,0:T(8,128)(2,1)S(1)}, bf16[128,2048]{1,0:T(8,128)(2,1)S(1)}, u32[]{:S(2)}, u32[]{:S(2)}) %collective-permute-start) | collective-permute-done | bytes 524320 | tf_op jit(solution)/shard_map/ppermute | solution.py:10
  205.1 0.0 copy-start.2
  205.1 0.8 copy-done.2
  205.9 0.0 all-to-all-done.1
  205.9 0.9 bitcast_select_fusion
  206.8 1.9 copy.9
  (3 shorter events, 0.0 us)
Async XLA Ops:
  7.2 61.7 %copy-start = (bf16[1,512,2048]{2,1,0:T(8,128)(2,1)S(1)}, bf16[1,512,2048]{2,1,0:T(8,128)(2,1)}, u32[]{:S(2)}) copy-start(bf16[1,512,2048]{2,1,0:T(8,128)(2,1)} %param.7) | copy-start | bytes 6291460
  7.2 61.7 %all-gather.3.cloned.1.call-start = ((), (), s32[]{:S(2)}) async-start(), calls=%async_computation.4 | async-start | bytes 2621440 | tf_op jit(solution)/shard_map/all_gather | solution.py:14
  7.9 153.3 %reduce-scatter.2.cloned.1.call-start = ((), (), s32[]{:S(2)}) async-start(), calls=%async_computation.3 | async-start | bytes 8912896 | tf_op jit(solution)/shard_map/reduce_scatter | solution.py:18
  77.3 83.9 %copy-start.1 = (bf16[1,128,2048]{2,1,0:T(8,128)(2,1)S(1)}, bf16[1,128,2048]{2,1,0:T(8,128)(2,1)}, u32[]{:S(2)}) copy-start(bf16[1,128,2048]{2,1,0:T(8,128)(2,1)} %param.6) | copy-start | bytes 1572868
  77.3 92.2 %copy-start.3 = (f32[1,8192]{1,0:T(1,128)S(1)}, f32[1,8192]{1,0:T(1,128)}, u32[]{:S(2)}) copy-start(f32[1,8192]{1,0:T(1,128)} %param.8) | copy-start | bytes 98308
  163.2 20.3 %all-to-all-start = ((bf16[4,32,2048]{2,1,0:T(8,128)(2,1)}), bf16[4,32,2048]{2,1,0:T(8,128)(2,1)S(1)}, u32[]{:S(2)}, u32[]{:S(2)}) async-start(bf16[4,32,2048]{2,1,0:T(8,128)(2,1)} %bitcast.4), calls=%async_computation.1 | async-start | bytes 1048576 | tf_op jit(solution)/shard_map/all_to_all | solution.py:25
  184.7 21.1 %all-to-all-start.1 = ((bf16[32,4,2048]{2,0,1:T(8,128)(2,1)}), bf16[32,4,2048]{2,0,1:T(8,128)(2,1)S(1)}, u32[]{:S(2)}, u32[]{:S(2)}) async-start(bf16[32,4,2048]{2,0,1:T(8,128)(2,1)} %fusion.6), calls=%async_computation.2 | async-start | bytes 1048576 | tf_op jit(solution)/shard_map/all_to_all | solution.py:30
  188.9 16.2 %collective-permute-start = (bf16[128,2048]{1,0:T(8,128)(2,1)S(1)}, bf16[128,2048]{1,0:T(8,128)(2,1)S(1)}, u32[]{:S(2)}, u32[]{:S(2)}) collective-permute-start(bf16[128,2048]{1,0:T(8,128)(2,1)S(1)} %get-tuple-element.2), channel_id=1, source_target_pairs={{0,64},{64,128},{128,192},{192,256},{256,320},{320,384},{384,448},... | collective-permute-start | bytes 1572872 | tf_op jit(solution)/shard_map/ppermute | solution.py:10
  205.1 0.8 copy-start.2
Sparse Core Ops, SparseCore 0:
  10.4 58.4 all-gather.2
  77.4 83.7 reduce-scatter.1
where the time goes:
time: 216 us; the launch traced here: 215 us
  waiting for transfers between devices  170 us (79%)
  between operations  14.8 us (7%)
  starting transfers between devices  14.5 us (7%)
  matrix products  8.39 us (4%)
  other arithmetic  4.9 us (2%)
  local copies, waits for them, and re-layouts  3.22 us (1%)
    reduce_scatter x1, waiting for transfers between devices, on_device(): lax.psum_scatter(jnp.dot(whole, weight, preferred_element_type=jnp.float3...  83.1 us
    all_gather x1, waiting for transfers between devices, on_device(): whole = lax.all_gather(context[0], 'dp', axis=0, tiled=True)  60.9 us
    all_to_all x1, waiting for transfers between devices, on_device(): lax.all_to_all(hidden.astype(jnp.bfloat16), 'dp', split_axis=0, concat_ax...  13.2 us
    ppermute x1, waiting for transfers between devices, passed_along(): lax.ppermute(value, axis, [(source, source + steps) for source in range(l...  11.7 us
    dot_general x1, matrix products, on_device(): jnp.dot(whole, weight, preferred_element_type=jnp.float32)  8.39 us
    all_to_all x1, starting transfers between devices, on_device(): lax.all_to_all(hidden.astype(jnp.bfloat16), 'dp', split_axis=0, concat_ax...  5.85 us
    ppermute x1, starting transfers between devices, passed_along(): lax.ppermute(value, axis, [(source, source + steps) for source in range(l...  4.44 us
  transfers between devices with their start and end apart: 5, of which 4 were waited for; matrix products, arithmetic and copies ran while one was open for 1% of the time, Pallas kernels for 0%

commit v1 on v0

v1 whole, which is shorter than its diff:
```python
import functools

import jax
import jax.numpy as jnp
from jax import lax
from jax.experimental import pallas as pl
from jax.experimental.pallas import tpu as pltpu
from jax.sharding import Mesh, PartitionSpec as P

CHUNKS = 2
HALF = 1024
WIDE = 256


def project(pos, own, right, left, far_r, far_l, w_own, w_oth, w_own_b, w_oth_b, keep_a, send_a, keep_b, send_b, rows_a, rows_b):
    step = pl.program_id(0)

    @pl.when(step == 0)
    def _():
        d, x = pos[0], pos[1]
        outer = jnp.logical_or(x == 0, x == 3).astype(jnp.int32)
        for source, shift, xls in ((own, 0, (0, 1)), (right, 3, (0, 1)), (left, 1, (0, 1)), (far_r, 2, (0,)), (far_l, 2, (1,))):
            dd = lax.rem(d + shift, 4)
            odd, ylo = dd % 2, dd // 2
            for xl in xls:
                block = source[xl] if len(xls) == 2 else source[...]
                same = (odd == xl).astype(jnp.int32)
                slot_a = jnp.where(same == outer, 0, 4) + odd * 2 + ylo
                slot_b = jnp.where(odd == x // 2, 0, 4) + xl * 2 + ylo
                rows_a[slot_a] = block
                rows_b[slot_b] = block

    for rows, first, second, keep, send in ((rows_a, w_own, w_oth, keep_a, send_a), (rows_b, w_own_b, w_oth_b, keep_b, send_b)):
        lhs = rows[...].reshape(-1, 2 * w_own.shape[0])
        k = w_own.shape[0]
        value = jnp.dot(lhs[:, :k], first[...], preferred_element_type=jnp.float32)
        value += jnp.dot(lhs[:, k:], second[...], preferred_element_type=jnp.float32)
        value = value.astype(jnp.bfloat16)
        half = value.shape[0] // 2
        keep[...] = value[:half]
        send[...] = value[half:]


def projected(pos, own, right, left, far_r, far_l, w_own, w_oth):
    r, k2 = own.shape[1], own.shape[2]
    k = k2 // 2
    whole = lambda a: pl.BlockSpec(a.shape, lambda j, p: (0,) * a.ndim)
    tile = lambda off: pl.BlockSpec((k, WIDE), lambda j, p: (0, j + off))
    steps = HALF // WIDE
    out = jax.ShapeDtypeStruct((4 * r, HALF), jnp.bfloat16)
    return pl.pallas_call(
        project,
        grid_spec=pltpu.PrefetchScalarGridSpec(
            num_scalar_prefetch=1,
            grid=(steps,),
            in_specs=[whole(own), whole(right), whole(left), whole(far_r), whole(far_l), tile(0), tile(0), tile(steps), tile(steps)],
            out_specs=[pl.BlockSpec((4 * r, WIDE), lambda j, p: (0, j))] * 4,
            scratch_shapes=[pltpu.VMEM((8, r, k2), jnp.bfloat16)] * 2,
        ),
        out_shape=[out] * 4,
        cost_estimate=pl.CostEstimate(flops=2 * 8 * r * k2 * 2 * HALF, bytes_accessed=2 * (8 * r * k2 + 2 * k2 * HALF + 16 * r * HALF), transcendentals=0),
        compiler_params=pltpu.CompilerParams(vmem_limit_bytes=40 * 2**20),
    )(pos, own, right, left, far_r, far_l, w_own, w_oth, w_own, w_oth)


def split_sum(pos, keep_a, got_a, keep_b, got_b, mine_a, give_a, mine_b, give_b):
    x = pos[1]
    for keep, got, mine, give, rank in ((keep_a, got_a, mine_a, give_a, x // 2), (keep_b, got_b, mine_b, give_b, x % 2)):
        mine[...] = (keep[rank].astype(jnp.float32) + got[rank].astype(jnp.float32)).astype(jnp.bfloat16)
        give[...] = (keep[1 - rank].astype(jnp.float32) + got[1 - rank].astype(jnp.float32)).astype(jnp.bfloat16)


def split_summed(pos, keep_a, got_a, keep_b, got_b):
    n, m = keep_a.shape
    args = [a.reshape(2, n // 2, m) for a in (keep_a, got_a, keep_b, got_b)]
    vmem = pl.BlockSpec(memory_space=pltpu.VMEM)
    return pl.pallas_call(
        split_sum,
        in_specs=[pl.BlockSpec(memory_space=pltpu.SMEM)] + [vmem] * 4,
        out_specs=[vmem] * 4,
        out_shape=[jax.ShapeDtypeStruct((n // 2, m), jnp.bfloat16)] * 4,
        cost_estimate=pl.CostEstimate(flops=2 * n * m, bytes_accessed=2 * n * m * 6, transcendentals=0),
    )(pos, *args)


def on_device(sections, context, residual, out_weight, norm_gain, valid_tokens):
    d, ylo, x, core = (lax.axis_index(a) for a in ("dp", "ylo", "x", "core"))
    pos = jnp.stack([d, x]).astype(jnp.int32)
    width = context.shape[2]
    rows = residual.shape[1]
    r = rows // CHUNKS
    ring = lambda k: [(i, (i + k) % 4) for i in range(4)]
    near, mirror, swap = [(i, i ^ 1) for i in range(4)], [(i, 3 - i) for i in range(4)], [(0, 1), (1, 0)]

    tokens = context.reshape(2, 2, rows, width)
    mine = lax.dynamic_index_in_dim(tokens, core, 1, keepdims=False)
    theirs = lax.dynamic_index_in_dim(tokens, 1 - core, 1, keepdims=False)
    both = jnp.concatenate([mine, lax.ppermute(theirs, "core", swap)], axis=-1)
    w_own = out_weight[0]
    w_oth = lax.ppermute(w_own, "core", swap)

    outs, squares, moved = [], [], []
    hs = []
    for c in range(CHUNKS):
        own = both[:, c * r:(c + 1) * r]
        right = lax.ppermute(own, "dp", ring(1))
        left = lax.ppermute(own, "dp", ring(3))
        far_r = lax.ppermute(right[0], "dp", ring(1))
        far_l = lax.ppermute(left[1], "dp", ring(3))
        keep_a, send_a, keep_b, send_b = projected(pos, own, right, left, far_r, far_l, w_own, w_oth)
        got_a = lax.ppermute(send_a, "x", near)
        got_b = lax.ppermute(send_b, "x", mirror)
        keep_a, send_a, keep_b, send_b = split_summed(pos, keep_a, got_a, keep_b, got_b)
        got_a = lax.ppermute(send_a, "x", mirror)
        got_b = lax.ppermute(send_b, "x", near)
        total = jnp.concatenate([
            (keep_a.astype(jnp.float32) + got_a.astype(jnp.float32)).reshape(2, r, HALF),
            (keep_b.astype(jnp.float32) + got_b.astype(jnp.float32)).reshape(2, r, HALF)], axis=-1)
        stay = lax.dynamic_index_in_dim(total, ylo, 0, keepdims=False)
        go = lax.dynamic_index_in_dim(total, 1 - ylo, 0, keepdims=False).astype(jnp.bfloat16)
        attn = stay + lax.ppermute(go, "ylo", swap).astype(jnp.float32)
        h = residual[0, c * r:(c + 1) * r].astype(jnp.float32) + attn
        row = ((ylo * 4 + x) * 2 + core) * rows + c * r + jnp.arange(r, dtype=jnp.int32)
        live = (row < valid_tokens[0])[:, None]
        out = jnp.where(live, h, 0.0).astype(jnp.bfloat16)
        moved.append(lax.ppermute(out, "section", [(s, s + 1) for s in range(sections - 1)]))
        hs.append(jnp.where(live, h, 0.0))
        squares.append(jnp.sum(h * h, axis=1))
    square = jnp.concatenate(squares)[None]
    square = square + lax.ppermute(square, "dp", near)
    square = square + lax.ppermute(square, "dp", [(i, i ^ 2) for i in range(4)])
    scale = lax.rsqrt(square[0] / 8192.0 + 1e-06)
    gain = lax.dynamic_slice_in_dim(norm_gain[0], d * residual.shape[2], residual.shape[2])
    normed = (jnp.concatenate(hs) * scale[:, None] * gain[None, :]).astype(jnp.bfloat16)
    return normed[None], jnp.concatenate(moved)[None]


def solution(mesh):
    sections = mesh.devices.shape[0]
    fine = Mesh(mesh.devices.reshape(sections, 4, 2, 4, 2), ("section", "dp", "ylo", "x", "core"))
    tensor = ("ylo", "x", "core")
    placed = (P("section", "dp", tensor), P("section", tensor, "dp"), P("section", tensor, "dp"), P("section", None), P("section"))
    return jax.shard_map(
        functools.partial(on_device, sections),
        mesh=fine,
        in_specs=placed,
        out_specs=(P("section", tensor, "dp"), P("section", tensor, "dp")),
        check_vma=False,
    )
```

time: 216 us -> 143 us (0.66)
  the two profiles are of different devices: /device:TPU:71 before, /device:TPU:200 now
where the time goes in v1:
time: 143 us; the launch traced here: 142 us
  starting transfers between devices  83.3 us (58%)
  waiting for transfers between devices  29.1 us (20%)
  Pallas kernels  16.1 us (11%)
  local copies, waits for them, and re-layouts  7.48 us (5%)
  other arithmetic  4.56 us (3%)
  between operations  1.84 us (1%)
    pallas_call x2, Pallas kernels, projected(): pl.pallas_call(project, grid_spec=pltpu.PrefetchScalarGridSpec(num_scalar...  10.7 us
    ppermute x2, starting transfers between devices, on_device(): lax.ppermute(out, 'section', [(s, s + 1) for s in range(sections - 1)])  9.77 us
    ppermute x2, starting transfers between devices, on_device(): far_l = lax.ppermute(left[1], 'dp', ring(3))  8.7 us
    ppermute x2, waiting for transfers between devices, on_device(): right = lax.ppermute(own, 'dp', ring(1))  8.55 us
    ppermute x2, starting transfers between devices, on_device(): left = lax.ppermute(own, 'dp', ring(3))  8.12 us
    ppermute x2, starting transfers between devices, on_device(): right = lax.ppermute(own, 'dp', ring(1))  7.79 us
    ppermute x2, starting transfers between devices, on_device(): got_a = lax.ppermute(send_a, 'x', mirror)  7.29 us
    ppermute x2, starting transfers between devices, on_device(): far_r = lax.ppermute(right[0], 'dp', ring(1))  7.2 us
  transfers between devices with their start and end apart: 24, of which 10 were waited for; matrix products, arithmetic and copies ran while one was open for 2% of the time, Pallas kernels for 11%

profile of v1, /device:TPU:200, one launch (start us, length us, event | category | flops | bytes accessed | tf_op | source)
XLA Modules:
  0.0 142.4 jit_solution(12558012388486771791)
XLA Ops:
  0.7 2.1 %collective-permute-start.5 = (bf16[512,2048]{1,0:T(8,128)(2,1)}, bf16[512,2048]{1,0:T(8,128)(2,1)}, u32[]{:S(2)}, u32[]{:S(2)}) collective-permute-start(bf16[512,2048]{1,0:T(8,128)(2,1)} %bitcast.73), channel_id=1, source_target_pairs={{0,1},{1,0},{2,3},{3,2},{4,5},{5,4},{6,7},{7,6},{8,9},{9,8},{10,11... | collective-permute-start | bytes 6291464 | tf_op jit(solution)/shard_map/ppermute | solution.py:100
  2.7 1.1 dynamic-slice_bitcast_fusion.1
  3.8 2.4 %collective-permute-start = (bf16[2,128,512]{2,1,0:T(8,128)(2,1)S(1)}, bf16[2,128,512]{2,1,0:T(8,128)(2,1)S(1)}, u32[]{:S(2)}, u32[]{:S(2)}) collective-permute-start(bf16[2,128,512]{2,1,0:T(8,128)(2,1)S(1)} %get-tuple-element.47), channel_id=1, source_target_pairs={{0,1},{1,0},{2,3},{3,2},{4,5},{5,4},{6,7},{7,6},{8,9},{9,8},{10,11... | collective-permute-start | bytes 786440 | tf_op jit(solution)/shard_map/ppermute | solution.py:98
  6.2 1.1 collective-permute-done
  7.4 4.5 %collective-permute-start.11 = (bf16[2,64,1024]{2,1,0:T(8,128)(2,1)S(1)}, bf16[2,64,1024]{2,1,0:T(8,128)(2,1)S(1)}, u32[]{:S(2)}, u32[]{:S(2)}) collective-permute-start(bf16[2,64,1024]{2,1,0:T(8,128)(2,1)S(1)} %get-tuple-element.45.own), channel_id=1, source_target_pairs={{0,16},{16,32},{32,48},{48,0},{1,17},{17,33},{33,49},{49,1},{2,18}... | collective-permute-start | bytes 786440 | tf_op jit(solution)/shard_map/ppermute | solution.py:106
  11.9 3.5 %collective-permute-start.12 = (bf16[2,64,1024]{2,1,0:T(8,128)(2,1)S(1)}, bf16[2,64,1024]{2,1,0:T(8,128)(2,1)S(1)}, u32[]{:S(2)}, u32[]{:S(2)}) collective-permute-start(bf16[2,64,1024]{2,1,0:T(8,128)(2,1)S(1)} %get-tuple-element.45.own), channel_id=1, source_target_pairs={{0,48},{16,0},{32,16},{48,32},{1,49},{17,1},{33,17},{49,33},{2,50}... | collective-permute-start | bytes 786440 | tf_op jit(solution)/shard_map/ppermute | solution.py:107
  15.5 3.3 %collective-permute-start.1 = (bf16[2,64,1024]{2,1,0:T(8,128)(2,1)S(1)}, bf16[2,64,1024]{2,1,0:T(8,128)(2,1)S(1)}, u32[]{:S(2)}, u32[]{:S(2)}) collective-permute-start(bf16[2,64,1024]{2,1,0:T(8,128)(2,1)S(1)} %get-tuple-element.44.own), channel_id=1, source_target_pairs={{0,16},{16,32},{32,48},{48,0},{1,17},{17,33},{33,49},{49,1},{2,18}... | collective-permute-start | bytes 786440 | tf_op jit(solution)/shard_map/ppermute | solution.py:106
  18.8 4.7 %collective-permute-start.2 = (bf16[2,64,1024]{2,1,0:T(8,128)(2,1)S(1)}, bf16[2,64,1024]{2,1,0:T(8,128)(2,1)S(1)}, u32[]{:S(2)}, u32[]{:S(2)}) collective-permute-start(bf16[2,64,1024]{2,1,0:T(8,128)(2,1)S(1)} %get-tuple-element.44.own), channel_id=1, source_target_pairs={{0,48},{16,0},{32,16},{48,32},{1,49},{17,1},{33,17},{49,33},{2,50}... | collective-permute-start | bytes 786440 | tf_op jit(solution)/shard_map/ppermute | solution.py:107
  23.4 6.4 %collective-permute-done.11.right = bf16[2,64,1024]{2,1,0:T(8,128)(2,1)S(1)} collective-permute-done((bf16[2,64,1024]{2,1,0:T(8,128)(2,1)S(1)}, bf16[2,64,1024]{2,1,0:T(8,128)(2,1)S(1)}, u32[]{:S(2)}, u32[]{:S(2)}) %collective-permute-start.11) | collective-permute-done | bytes 262176 | tf_op jit(solution)/shard_map/ppermute | solution.py:106
  29.9 4.0 %collective-permute-start.13 = (bf16[64,1024]{1,0:T(8,128)(2,1)S(1)}, bf16[64,1024]{1,0:T(8,128)(2,1)S(1)}, u32[]{:S(2)}, u32[]{:S(2)}) collective-permute-start(bf16[64,1024]{1,0:T(8,128)(2,1)S(1)} %slice_bitcast_fusion.1), channel_id=1, source_target_pairs={{0,16},{16,32},{32,48},{48,0},{1,17},{17,33},{33,49},{49,1},{2,18}... | collective-permute-start | bytes 393224 | tf_op jit(solution)/shard_map/ppermute | solution.py:108
  33.9 3.9 %collective-permute-start.14 = (bf16[64,1024]{1,0:T(8,128)(2,1)S(1)}, bf16[64,1024]{1,0:T(8,128)(2,1)S(1)}, u32[]{:S(2)}, u32[]{:S(2)}) collective-permute-start(bf16[64,1024]{1,0:T(8,128)(2,1)S(1)} %slice_bitcast_fusion), channel_id=1, source_target_pairs={{0,48},{16,0},{32,16},{48,32},{1,49},{17,1},{33,17},{49,33},{2,50}... | collective-permute-start | bytes 393224 | tf_op jit(solution)/shard_map/ppermute | solution.py:109
  37.9 2.1 %collective-permute-done.1.right = bf16[2,64,1024]{2,1,0:T(8,128)(2,1)S(1)} collective-permute-done((bf16[2,64,1024]{2,1,0:T(8,128)(2,1)S(1)}, bf16[2,64,1024]{2,1,0:T(8,128)(2,1)S(1)}, u32[]{:S(2)}, u32[]{:S(2)}) %collective-permute-start.1) | collective-permute-done | bytes 262176 | tf_op jit(solution)/shard_map/ppermute | solution.py:106
  40.0 3.2 %collective-permute-start.3 = (bf16[64,1024]{1,0:T(8,128)(2,1)S(1)}, bf16[64,1024]{1,0:T(8,128)(2,1)S(1)}, u32[]{:S(2)}, u32[]{:S(2)}) collective-permute-start(bf16[64,1024]{1,0:T(8,128)(2,1)S(1)} %slice_bitcast_fusion.3), channel_id=1, source_target_pairs={{0,16},{16,32},{32,48},{48,0},{1,17},{17,33},{33,49},{49,1},{2,18}... | collective-permute-start | bytes 393224 | tf_op jit(solution)/shard_map/ppermute | solution.py:108
  43.2 4.8 %collective-permute-start.4 = (bf16[64,1024]{1,0:T(8,128)(2,1)S(1)}, bf16[64,1024]{1,0:T(8,128)(2,1)S(1)}, u32[]{:S(2)}, u32[]{:S(2)}) collective-permute-start(bf16[64,1024]{1,0:T(8,128)(2,1)S(1)} %slice_bitcast_fusion.2), channel_id=1, source_target_pairs={{0,48},{16,0},{32,16},{48,32},{1,49},{17,1},{33,17},{49,33},{2,50}... | collective-permute-start | bytes 393224 | tf_op jit(solution)/shard_map/ppermute | solution.py:109
  48.1 5.3 %shard_map.70 = (bf16[256,1024]{1,0:T(8,128)(2,1)S(1)}, bf16[256,1024]{1,0:T(8,128)(2,1)S(1)}, bf16[256,1024]{1,0:T(8,128)(2,1)S(1)}, bf16[256,1024]{1,0:T(8,128)(2,1)S(1)}) custom-call(s32[2]{0:T(128)S(1)} %pad_add_fusion.pos, bf16[2,64,1024]{2,1,0:T(8,128)(2,1)S(1)} %get-tuple-element.45.own, bf16[2,64,1024]{2,1,0:T(8,128)(2,1)S(1)} %collective-permute-done.11.right, ...), custom_call_target="tpu_custom_call" | custom-call | flops 2147483648 | bytes 7340032 | tf_op jit(solution)/shard_map/pallas_call | solution.py:51
  53.4 0.8 copy-done.4
  54.2 0.8 copy-done.5
  55.0 3.4 %collective-permute-start.15 = (bf16[256,1024]{1,0:T(8,128)(2,1)S(1)}, bf16[256,1024]{1,0:T(8,128)(2,1)S(1)}, u32[]{:S(2)}, u32[]{:S(2)}) collective-permute-start(bf16[256,1024]{1,0:T(8,128)(2,1)S(1)} %get-tuple-element.27), channel_id=1, source_target_pairs={{0,2},{2,0},{4,6},{6,4},{1,3},{3,1},{5,7},{7,5},{8,10},{10,8},{12,... | collective-permute-start | bytes 1572872 | tf_op jit(solution)/shard_map/ppermute | solution.py:111
  58.4 4.0 %collective-permute-start.16 = (bf16[256,1024]{1,0:T(8,128)(2,1)S(1)}, bf16[256,1024]{1,0:T(8,128)(2,1)S(1)}, u32[]{:S(2)}, u32[]{:S(2)}) collective-permute-start(bf16[256,1024]{1,0:T(8,128)(2,1)S(1)} %get-tuple-element.29), channel_id=1, source_target_pairs={{0,6},{2,4},{4,2},{6,0},{1,7},{3,5},{5,3},{7,1},{8,14},{10,12},{12... | collective-permute-start | bytes 1572872 | tf_op jit(solution)/shard_map/ppermute | solution.py:112
  62.5 5.3 %shard_map.68 = (bf16[256,1024]{1,0:T(8,128)(2,1)S(1)}, bf16[256,1024]{1,0:T(8,128)(2,1)S(1)}, bf16[256,1024]{1,0:T(8,128)(2,1)S(1)}, bf16[256,1024]{1,0:T(8,128)(2,1)S(1)}) custom-call(s32[2]{0:T(128)S(1)} %pad_add_fusion.pos, bf16[2,64,1024]{2,1,0:T(8,128)(2,1)S(1)} %get-tuple-element.44.own, bf16[2,64,1024]{2,1,0:T(8,128)(2,1)S(1)} %collective-permute-done.1.right, ...), custom_call_target="tpu_custom_call" | custom-call | flops 2147483648 | bytes 7340032 | tf_op jit(solution)/shard_map/pallas_call | solution.py:51
  68.6 0.8 copy-done.3
  69.4 2.5 %collective-permute-start.6 = (bf16[256,1024]{1,0:T(8,128)(2,1)S(1)}, bf16[256,1024]{1,0:T(8,128)(2,1)S(1)}, u32[]{:S(2)}, u32[]{:S(2)}) collective-permute-start(bf16[256,1024]{1,0:T(8,128)(2,1)S(1)} %get-tuple-element.19), channel_id=1, source_target_pairs={{0,2},{2,0},{4,6},{6,4},{1,3},{3,1},{5,7},{7,5},{8,10},{10,8},{12,... | collective-permute-start | bytes 1572872 | tf_op jit(solution)/shard_map/ppermute | solution.py:111
  71.9 2.5 %collective-permute-start.7 = (bf16[256,1024]{1,0:T(8,128)(2,1)S(1)}, bf16[256,1024]{1,0:T(8,128)(2,1)S(1)}, u32[]{:S(2)}, u32[]{:S(2)}) collective-permute-start(bf16[256,1024]{1,0:T(8,128)(2,1)S(1)} %get-tuple-element.21), channel_id=1, source_target_pairs={{0,6},{2,4},{4,2},{6,0},{1,7},{3,5},{5,3},{7,1},{8,14},{10,12},{12... | collective-permute-start | bytes 1572872 | tf_op jit(solution)/shard_map/ppermute | solution.py:112
  74.5 0.8 copy-done.9
  75.3 0.8 copy-done.10
  76.1 2.7 %shard_map.71 = (bf16[128,1024]{1,0:T(8,128)(2,1)}, bf16[128,1024]{1,0:T(8,128)(2,1)}, bf16[128,1024]{1,0:T(8,128)(2,1)}, bf16[128,1024]{1,0:T(8,128)(2,1)}) custom-call(s32[2]{0:T(128)} %copy-done.6, bf16[2,128,1024]{2,1,0:T(8,128)(2,1)} %bitcast.80, bf16[2,128,1024]{2,1,0:T(8,128)(2,1)} %bitcast.92, bf16[2,128,1024]{2,1,0:T(8,128)(2,1)} %bitcast.81, ...), custom_call_target="tpu_custom_call" | custom-call | flops 524288 | bytes 3145728 | tf_op jit(solution)/shard_map/pallas_call | solution.py:77
  78.8 4.6 %collective-permute-start.17 = (bf16[128,1024]{1,0:T(8,128)(2,1)}, bf16[128,1024]{1,0:T(8,128)(2,1)S(1)}, u32[]{:S(2)}, u32[]{:S(2)}) collective-permute-start(bf16[128,1024]{1,0:T(8,128)(2,1)} %get-tuple-element.31), channel_id=1, source_target_pairs={{0,6},{2,4},{4,2},{6,0},{1,7},{3,5},{5,3},{7,1},{8,14},{10,12},{12... | collective-permute-start | bytes 786440 | tf_op jit(solution)/shard_map/ppermute | solution.py:114
  83.4 2.1 %collective-permute-start.18 = (bf16[128,1024]{1,0:T(8,128)(2,1)}, bf16[128,1024]{1,0:T(8,128)(2,1)S(1)}, u32[]{:S(2)}, u32[]{:S(2)}) collective-permute-start(bf16[128,1024]{1,0:T(8,128)(2,1)} %get-tuple-element.33), channel_id=1, source_target_pairs={{0,2},{2,0},{4,6},{6,4},{1,3},{3,1},{5,7},{7,5},{8,10},{10,8},{12,... | collective-permute-start | bytes 786440 | tf_op jit(solution)/shard_map/ppermute | solution.py:115
  85.6 4.3 %collective-permute-done.7 = bf16[256,1024]{1,0:T(8,128)(2,1)S(1)} collective-permute-done((bf16[256,1024]{1,0:T(8,128)(2,1)S(1)}, bf16[256,1024]{1,0:T(8,128)(2,1)S(1)}, u32[]{:S(2)}, u32[]{:S(2)}) %collective-permute-start.7) | collective-permute-done | bytes 524320 | tf_op jit(solution)/shard_map/ppermute | solution.py:112
  89.9 0.8 copy-done.8
  90.7 2.7 %shard_map.69 = (bf16[128,1024]{1,0:T(8,128)(2,1)}, bf16[128,1024]{1,0:T(8,128)(2,1)}, bf16[128,1024]{1,0:T(8,128)(2,1)}, bf16[128,1024]{1,0:T(8,128)(2,1)}) custom-call(s32[2]{0:T(128)} %copy-done.6, bf16[2,128,1024]{2,1,0:T(8,128)(2,1)} %bitcast.78, bf16[2,128,1024]{2,1,0:T(8,128)(2,1)} %bitcast.90, bf16[2,128,1024]{2,1,0:T(8,128)(2,1)} %bitcast.79, ...), custom_call_target="tpu_custom_call" | custom-call | flops 524288 | bytes 3145728 | tf_op jit(solution)/shard_map/pallas_call | solution.py:77
  93.4 2.6 %collective-permute-start.8 = (bf16[128,1024]{1,0:T(8,128)(2,1)}, bf16[128,1024]{1,0:T(8,128)(2,1)S(1)}, u32[]{:S(2)}, u32[]{:S(2)}) collective-permute-start(bf16[128,1024]{1,0:T(8,128)(2,1)} %get-tuple-element.23), channel_id=1, source_target_pairs={{0,6},{2,4},{4,2},{6,0},{1,7},{3,5},{5,3},{7,1},{8,14},{10,12},{12... | collective-permute-start | bytes 786440 | tf_op jit(solution)/shard_map/ppermute | solution.py:114
  96.0 2.1 %collective-permute-start.9 = (bf16[128,1024]{1,0:T(8,128)(2,1)}, bf16[128,1024]{1,0:T(8,128)(2,1)S(1)}, u32[]{:S(2)}, u32[]{:S(2)}) collective-permute-start(bf16[128,1024]{1,0:T(8,128)(2,1)} %get-tuple-element.25), channel_id=1, source_target_pairs={{0,2},{2,0},{4,6},{6,4},{1,3},{3,1},{5,7},{7,5},{8,10},{10,8},{12,... | collective-permute-start | bytes 786440 | tf_op jit(solution)/shard_map/ppermute | solution.py:115
  98.3 2.1 %collective-permute-start.19 = (bf16[64,2048]{1,0:T(8,128)(2,1)S(1)}, bf16[64,2048]{1,0:T(8,128)(2,1)S(1)}, u32[]{:S(2)}, u32[]{:S(2)}) collective-permute-start(bf16[64,2048]{1,0:T(8,128)(2,1)S(1)} %fusion.16), channel_id=1, source_target_pairs={{0,8},{8,0},{1,9},{9,1},{2,10},{10,2},{3,11},{11,3},{4,12},{12,4},... | collective-permute-start | bytes 786440 | tf_op jit(solution)/shard_map/ppermute | solution.py:121
  100.4 2.8 %collective-permute-done.8 = bf16[128,1024]{1,0:T(8,128)(2,1)S(1)} collective-permute-done((bf16[128,1024]{1,0:T(8,128)(2,1)}, bf16[128,1024]{1,0:T(8,128)(2,1)S(1)}, u32[]{:S(2)}, u32[]{:S(2)}) %collective-permute-start.8) | collective-permute-done | bytes 262176 | tf_op jit(solution)/shard_map/ppermute | solution.py:114
  103.2 1.3 collective-permute-done.9
  105.3 1.9 %collective-permute-start.10 = (bf16[64,2048]{1,0:T(8,128)(2,1)}, bf16[64,2048]{1,0:T(8,128)(2,1)S(1)}, u32[]{:S(2)}, u32[]{:S(2)}) collective-permute-start(bf16[64,2048]{1,0:T(8,128)(2,1)} %fusion.15), channel_id=1, source_target_pairs={{0,8},{8,0},{1,9},{9,1},{2,10},{10,2},{3,11},{11,3},{4,12},{12,4},... | collective-permute-start | bytes 786440 | tf_op jit(solution)/shard_map/ppermute | solution.py:121
  107.9 1.4 %collective-permute-done.19 = bf16[64,2048]{1,0:T(8,128)(2,1)S(1)} collective-permute-done((bf16[64,2048]{1,0:T(8,128)(2,1)S(1)}, bf16[64,2048]{1,0:T(8,128)(2,1)S(1)}, u32[]{:S(2)}, u32[]{:S(2)}) %collective-permute-start.19) | collective-permute-done | bytes 262176 | tf_op jit(solution)/shard_map/ppermute | solution.py:121
  109.3 4.4 %collective-permute-done.10 = bf16[64,2048]{1,0:T(8,128)(2,1)S(1)} collective-permute-done((bf16[64,2048]{1,0:T(8,128)(2,1)}, bf16[64,2048]{1,0:T(8,128)(2,1)S(1)}, u32[]{:S(2)}, u32[]{:S(2)}) %collective-permute-start.10) | collective-permute-done | bytes 262176 | tf_op jit(solution)/shard_map/ppermute | solution.py:121
  114.5 1.2 select_convert_fusion.1
  116.0 4.1 %collective-permute-start.20 = (f32[1,128]{1,0:T(1,128)S(1)}, f32[1,128]{1,0:T(1,128)S(1)}, u32[]{:S(2)}, u32[]{:S(2)}) collective-permute-start(f32[1,128]{1,0:T(1,128)S(1)} %maximum_bitcast_fusion.1), channel_id=1, source_target_pairs={{0,16},{16,0},{32,48},{48,32},{1,17},{17,1},{33,49},{49,33},{2,18}... | collective-permute-start | bytes 1544 | tf_op jit(solution)/shard_map/ppermute | solution.py:130
  120.2 2.2 %collective-permute-done.20 = f32[1,128]{1,0:T(1,128)S(1)} collective-permute-done((f32[1,128]{1,0:T(1,128)S(1)}, f32[1,128]{1,0:T(1,128)S(1)}, u32[]{:S(2)}, u32[]{:S(2)}) %collective-permute-start.20) | collective-permute-done | bytes 544 | tf_op jit(solution)/shard_map/ppermute | solution.py:130
  122.4 5.3 %collective-permute-start.21 = (f32[1,128]{1,0:T(1,128)S(1)}, f32[1,128]{1,0:T(1,128)S(1)}, u32[]{:S(2)}, u32[]{:S(2)}) collective-permute-start(f32[1,128]{1,0:T(1,128)S(1)} %fusion.19), channel_id=1, source_target_pairs={{0,32},{16,48},{32,0},{48,16},{1,33},{17,49},{33,1},{49,17},{2,34}... | collective-permute-start | bytes 1544 | tf_op jit(solution)/shard_map/ppermute | solution.py:131
  127.8 5.5 %collective-permute-start.22 = (bf16[64,2048]{1,0:T(8,128)(2,1)S(1)}, bf16[64,2048]{1,0:T(8,128)(2,1)S(1)}, u32[]{:S(2)}, u32[]{:S(2)}) collective-permute-start(bf16[64,2048]{1,0:T(8,128)(2,1)S(1)} %get-tuple-element.34), channel_id=1, source_target_pairs={{0,64},{64,128},{128,192},{192,256},{256,320},{320,384},{384,448},... | collective-permute-start | bytes 786440 | tf_op jit(solution)/shard_map/ppermute | solution.py:126
  133.3 4.3 %collective-permute-start.23 = (bf16[64,2048]{1,0:T(8,128)(2,1)S(1)}, bf16[64,2048]{1,0:T(8,128)(2,1)S(1)}, u32[]{:S(2)}, u32[]{:S(2)}) collective-permute-start(bf16[64,2048]{1,0:T(8,128)(2,1)S(1)} %get-tuple-element.42), channel_id=1, source_target_pairs={{0,64},{64,128},{128,192},{192,256},{256,320},{320,384},{384,448},... | collective-permute-start | bytes 786440 | tf_op jit(solution)/shard_map/ppermute | solution.py:126
  137.6 0.9 fusion.1
  138.6 3.0 %collective-permute-done.23 = bf16[64,2048]{1,0:T(8,128)(2,1)S(1)} collective-permute-done((bf16[64,2048]{1,0:T(8,128)(2,1)S(1)}, bf16[64,2048]{1,0:T(8,128)(2,1)S(1)}, u32[]{:S(2)}, u32[]{:S(2)}) %collective-permute-start.23) | collective-permute-done | bytes 262176 | tf_op jit(solution)/shard_map/ppermute | solution.py:126
  141.6 0.8 maximum_bitcast_fusion
  (61 shorter events, 3.2 us)
Async XLA Ops:
  0.6 127.1 %copy-start = (f32[1,8192]{1,0:T(1,128)S(1)}, f32[1,8192]{1,0:T(1,128)}, u32[]{:S(2)}) copy-start(f32[1,8192]{1,0:T(1,128)} %param.8) | copy-start | bytes 98308
  0.6 47.4 %copy-start.1 = (bf16[1,512,2048]{2,1,0:T(8,128)(2,1)S(1)}, bf16[1,512,2048]{2,1,0:T(8,128)(2,1)}, u32[]{:S(2)}) copy-start(bf16[1,512,2048]{2,1,0:T(8,128)(2,1)} %param.7) | copy-start | bytes 6291460
  0.7 47.4 %collective-permute-start.5 = (bf16[512,2048]{1,0:T(8,128)(2,1)}, bf16[512,2048]{1,0:T(8,128)(2,1)}, u32[]{:S(2)}, u32[]{:S(2)}) collective-permute-start(bf16[512,2048]{1,0:T(8,128)(2,1)} %bitcast.73), channel_id=1, source_target_pairs={{0,1},{1,0},{2,3},{3,2},{4,5},{5,4},{6,7},{7,6},{8,9},{9,8},{10,11... | collective-permute-start | bytes 6291464 | tf_op jit(solution)/shard_map/ppermute | solution.py:100
  3.8 3.6 %collective-permute-start = (bf16[2,128,512]{2,1,0:T(8,128)(2,1)S(1)}, bf16[2,128,512]{2,1,0:T(8,128)(2,1)S(1)}, u32[]{:S(2)}, u32[]{:S(2)}) collective-permute-start(bf16[2,128,512]{2,1,0:T(8,128)(2,1)S(1)} %get-tuple-element.47), channel_id=1, source_target_pairs={{0,1},{1,0},{2,3},{3,2},{4,5},{5,4},{6,7},{7,6},{8,9},{9,8},{10,11... | collective-permute-start | bytes 786440 | tf_op jit(solution)/shard_map/ppermute | solution.py:98
  7.4 22.4 %collective-permute-start.11 = (bf16[2,64,1024]{2,1,0:T(8,128)(2,1)S(1)}, bf16[2,64,1024]{2,1,0:T(8,128)(2,1)S(1)}, u32[]{:S(2)}, u32[]{:S(2)}) collective-permute-start(bf16[2,64,1024]{2,1,0:T(8,128)(2,1)S(1)} %get-tuple-element.45.own), channel_id=1, source_target_pairs={{0,16},{16,32},{32,48},{48,0},{1,17},{17,33},{33,49},{49,1},{2,18}... | collective-permute-start | bytes 786440 | tf_op jit(solution)/shard_map/ppermute | solution.py:106
  11.9 22.0 %collective-permute-start.12 = (bf16[2,64,1024]{2,1,0:T(8,128)(2,1)S(1)}, bf16[2,64,1024]{2,1,0:T(8,128)(2,1)S(1)}, u32[]{:S(2)}, u32[]{:S(2)}) collective-permute-start(bf16[2,64,1024]{2,1,0:T(8,128)(2,1)S(1)} %get-tuple-element.45.own), channel_id=1, source_target_pairs={{0,48},{16,0},{32,16},{48,32},{1,49},{17,1},{33,17},{49,33},{2,50}... | collective-permute-start | bytes 786440 | tf_op jit(solution)/shard_map/ppermute | solution.py:107
  15.5 47.0 %copy-start.6 = (s32[2]{0:T(128)}, s32[2]{0:T(128)S(1)}, u32[]{:S(2)}) copy-start(s32[2]{0:T(128)S(1)} %pad_add_fusion.pos) | copy-start | bytes 28
  15.5 24.5 %collective-permute-start.1 = (bf16[2,64,1024]{2,1,0:T(8,128)(2,1)S(1)}, bf16[2,64,1024]{2,1,0:T(8,128)(2,1)S(1)}, u32[]{:S(2)}, u32[]{:S(2)}) collective-permute-start(bf16[2,64,1024]{2,1,0:T(8,128)(2,1)S(1)} %get-tuple-element.44.own), channel_id=1, source_target_pairs={{0,16},{16,32},{32,48},{48,0},{1,17},{17,33},{33,49},{49,1},{2,18}... | collective-permute-start | bytes 786440 | tf_op jit(solution)/shard_map/ppermute | solution.py:106
  18.8 24.4 %collective-permute-start.2 = (bf16[2,64,1024]{2,1,0:T(8,128)(2,1)S(1)}, bf16[2,64,1024]{2,1,0:T(8,128)(2,1)S(1)}, u32[]{:S(2)}, u32[]{:S(2)}) collective-permute-start(bf16[2,64,1024]{2,1,0:T(8,128)(2,1)S(1)} %get-tuple-element.44.own), channel_id=1, source_target_pairs={{0,48},{16,0},{32,16},{48,32},{1,49},{17,1},{33,17},{49,33},{2,50}... | collective-permute-start | bytes 786440 | tf_op jit(solution)/shard_map/ppermute | solution.py:107
  29.9 18.1 %collective-permute-start.13 = (bf16[64,1024]{1,0:T(8,128)(2,1)S(1)}, bf16[64,1024]{1,0:T(8,128)(2,1)S(1)}, u32[]{:S(2)}, u32[]{:S(2)}) collective-permute-start(bf16[64,1024]{1,0:T(8,128)(2,1)S(1)} %slice_bitcast_fusion.1), channel_id=1, source_target_pairs={{0,16},{16,32},{32,48},{48,0},{1,17},{17,33},{33,49},{49,1},{2,18}... | collective-permute-start | bytes 393224 | tf_op jit(solution)/shard_map/ppermute | solution.py:108
  33.9 14.1 %collective-permute-start.14 = (bf16[64,1024]{1,0:T(8,128)(2,1)S(1)}, bf16[64,1024]{1,0:T(8,128)(2,1)S(1)}, u32[]{:S(2)}, u32[]{:S(2)}) collective-permute-start(bf16[64,1024]{1,0:T(8,128)(2,1)S(1)} %slice_bitcast_fusion), channel_id=1, source_target_pairs={{0,48},{16,0},{32,16},{48,32},{1,49},{17,1},{33,17},{49,33},{2,50}... | collective-permute-start | bytes 393224 | tf_op jit(solution)/shard_map/ppermute | solution.py:109
  40.0 22.4 %collective-permute-start.3 = (bf16[64,1024]{1,0:T(8,128)(2,1)S(1)}, bf16[64,1024]{1,0:T(8,128)(2,1)S(1)}, u32[]{:S(2)}, u32[]{:S(2)}) collective-permute-start(bf16[64,1024]{1,0:T(8,128)(2,1)S(1)} %slice_bitcast_fusion.3), channel_id=1, source_target_pairs={{0,16},{16,32},{32,48},{48,0},{1,17},{17,33},{33,49},{49,1},{2,18}... | collective-permute-start | bytes 393224 | tf_op jit(solution)/shard_map/ppermute | solution.py:108
  43.2 19.2 %collective-permute-start.4 = (bf16[64,1024]{1,0:T(8,128)(2,1)S(1)}, bf16[64,1024]{1,0:T(8,128)(2,1)S(1)}, u32[]{:S(2)}, u32[]{:S(2)}) collective-permute-start(bf16[64,1024]{1,0:T(8,128)(2,1)S(1)} %slice_bitcast_fusion.2), channel_id=1, source_target_pairs={{0,48},{16,0},{32,16},{48,32},{1,49},{17,1},{33,17},{49,33},{2,50}... | collective-permute-start | bytes 393224 | tf_op jit(solution)/shard_map/ppermute | solution.py:109
  53.4 0.8 copy-start.4
  54.2 0.8 copy-start.5
  55.0 19.4 %collective-permute-start.15 = (bf16[256,1024]{1,0:T(8,128)(2,1)S(1)}, bf16[256,1024]{1,0:T(8,128)(2,1)S(1)}, u32[]{:S(2)}, u32[]{:S(2)}) collective-permute-start(bf16[256,1024]{1,0:T(8,128)(2,1)S(1)} %get-tuple-element.27), channel_id=1, source_target_pairs={{0,2},{2,0},{4,6},{6,4},{1,3},{3,1},{5,7},{7,5},{8,10},{10,8},{12,... | collective-permute-start | bytes 1572872 | tf_op jit(solution)/shard_map/ppermute | solution.py:111
  58.4 16.0 %collective-permute-start.16 = (bf16[256,1024]{1,0:T(8,128)(2,1)S(1)}, bf16[256,1024]{1,0:T(8,128)(2,1)S(1)}, u32[]{:S(2)}, u32[]{:S(2)}) collective-permute-start(bf16[256,1024]{1,0:T(8,128)(2,1)S(1)} %get-tuple-element.29), channel_id=1, source_target_pairs={{0,6},{2,4},{4,2},{6,0},{1,7},{3,5},{5,3},{7,1},{8,14},{10,12},{12... | collective-permute-start | bytes 1572872 | tf_op jit(solution)/shard_map/ppermute | solution.py:112
  67.8 0.8 copy-start.2
  68.6 0.8 copy-start.3
  69.4 16.2 %collective-permute-start.6 = (bf16[256,1024]{1,0:T(8,128)(2,1)S(1)}, bf16[256,1024]{1,0:T(8,128)(2,1)S(1)}, u32[]{:S(2)}, u32[]{:S(2)}) collective-permute-start(bf16[256,1024]{1,0:T(8,128)(2,1)S(1)} %get-tuple-element.19), channel_id=1, source_target_pairs={{0,2},{2,0},{4,6},{6,4},{1,3},{3,1},{5,7},{7,5},{8,10},{10,8},{12,... | collective-permute-start | bytes 1572872 | tf_op jit(solution)/shard_map/ppermute | solution.py:111
  71.9 18.0 %collective-permute-start.7 = (bf16[256,1024]{1,0:T(8,128)(2,1)S(1)}, bf16[256,1024]{1,0:T(8,128)(2,1)S(1)}, u32[]{:S(2)}, u32[]{:S(2)}) collective-permute-start(bf16[256,1024]{1,0:T(8,128)(2,1)S(1)} %get-tuple-element.21), channel_id=1, source_target_pairs={{0,6},{2,4},{4,2},{6,0},{1,7},{3,5},{5,3},{7,1},{8,14},{10,12},{12... | collective-permute-start | bytes 1572872 | tf_op jit(solution)/shard_map/ppermute | solution.py:112
  74.4 0.8 copy-start.9
  75.3 0.8 copy-start.10
  78.8 19.3 %copy-start.14 = (bf16[128,1024]{1,0:T(8,128)(2,1)S(1)}, bf16[128,1024]{1,0:T(8,128)(2,1)}, u32[]{:S(2)}) copy-start(bf16[128,1024]{1,0:T(8,128)(2,1)} %get-tuple-element.30) | copy-start | bytes 786436
  78.8 19.4 %copy-start.13 = (bf16[128,1024]{1,0:T(8,128)(2,1)S(1)}, bf16[128,1024]{1,0:T(8,128)(2,1)}, u32[]{:S(2)}) copy-start(bf16[128,1024]{1,0:T(8,128)(2,1)} %get-tuple-element.32) | copy-start | bytes 786436
  78.8 19.3 %collective-permute-start.17 = (bf16[128,1024]{1,0:T(8,128)(2,1)}, bf16[128,1024]{1,0:T(8,128)(2,1)S(1)}, u32[]{:S(2)}, u32[]{:S(2)}) collective-permute-start(bf16[128,1024]{1,0:T(8,128)(2,1)} %get-tuple-element.31), channel_id=1, source_target_pairs={{0,6},{2,4},{4,2},{6,0},{1,7},{3,5},{5,3},{7,1},{8,14},{10,12},{12... | collective-permute-start | bytes 786440 | tf_op jit(solution)/shard_map/ppermute | solution.py:114
  83.4 14.8 %collective-permute-start.18 = (bf16[128,1024]{1,0:T(8,128)(2,1)}, bf16[128,1024]{1,0:T(8,128)(2,1)S(1)}, u32[]{:S(2)}, u32[]{:S(2)}) collective-permute-start(bf16[128,1024]{1,0:T(8,128)(2,1)} %get-tuple-element.33), channel_id=1, source_target_pairs={{0,2},{2,0},{4,6},{6,4},{1,3},{3,1},{5,7},{7,5},{8,10},{10,8},{12,... | collective-permute-start | bytes 786440 | tf_op jit(solution)/shard_map/ppermute | solution.py:115
  85.6 4.3 %copy-start.7 = (bf16[256,1024]{1,0:T(8,128)(2,1)}, bf16[256,1024]{1,0:T(8,128)(2,1)S(1)}, u32[]{:S(2)}) copy-start(bf16[256,1024]{1,0:T(8,128)(2,1)S(1)} %collective-permute-done.6) | copy-start | bytes 1572868
  89.9 0.8 copy-start.8
  93.4 9.8 %copy-start.16 = (bf16[128,1024]{1,0:T(8,128)(2,1)S(1)}, bf16[128,1024]{1,0:T(8,128)(2,1)}, u32[]{:S(2)}) copy-start(bf16[128,1024]{1,0:T(8,128)(2,1)} %get-tuple-element.22) | copy-start | bytes 786436
  93.4 9.8 %collective-permute-start.8 = (bf16[128,1024]{1,0:T(8,128)(2,1)}, bf16[128,1024]{1,0:T(8,128)(2,1)S(1)}, u32[]{:S(2)}, u32[]{:S(2)}) collective-permute-start(bf16[128,1024]{1,0:T(8,128)(2,1)} %get-tuple-element.23), channel_id=1, source_target_pairs={{0,6},{2,4},{4,2},{6,0},{1,7},{3,5},{5,3},{7,1},{8,14},{10,12},{12... | collective-permute-start | bytes 786440 | tf_op jit(solution)/shard_map/ppermute | solution.py:114
  96.0 8.5 %collective-permute-start.9 = (bf16[128,1024]{1,0:T(8,128)(2,1)}, bf16[128,1024]{1,0:T(8,128)(2,1)S(1)}, u32[]{:S(2)}, u32[]{:S(2)}) collective-permute-start(bf16[128,1024]{1,0:T(8,128)(2,1)} %get-tuple-element.25), channel_id=1, source_target_pairs={{0,2},{2,0},{4,6},{6,4},{1,3},{3,1},{5,7},{7,5},{8,10},{10,8},{12,... | collective-permute-start | bytes 786440 | tf_op jit(solution)/shard_map/ppermute | solution.py:115
  98.1 6.4 %copy-start.15 = (bf16[128,1024]{1,0:T(8,128)(2,1)S(1)}, bf16[128,1024]{1,0:T(8,128)(2,1)}, u32[]{:S(2)}) copy-start(bf16[128,1024]{1,0:T(8,128)(2,1)} %get-tuple-element.24) | copy-start | bytes 786436
  98.3 16.2 %copy-start.11 = (bf16[1,128,2048]{2,1,0:T(8,128)(2,1)S(1)}, bf16[1,128,2048]{2,1,0:T(8,128)(2,1)}, u32[]{:S(2)}) copy-start(bf16[1,128,2048]{2,1,0:T(8,128)(2,1)} %param.6) | copy-start | bytes 1572868
  98.3 11.0 %collective-permute-start.19 = (bf16[64,2048]{1,0:T(8,128)(2,1)S(1)}, bf16[64,2048]{1,0:T(8,128)(2,1)S(1)}, u32[]{:S(2)}, u32[]{:S(2)}) collective-permute-start(bf16[64,2048]{1,0:T(8,128)(2,1)S(1)} %fusion.16), channel_id=1, source_target_pairs={{0,8},{8,0},{1,9},{9,1},{2,10},{10,2},{3,11},{11,3},{4,12},{12,4},... | collective-permute-start | bytes 786440 | tf_op jit(solution)/shard_map/ppermute | solution.py:121
  105.3 8.5 %collective-permute-start.10 = (bf16[64,2048]{1,0:T(8,128)(2,1)}, bf16[64,2048]{1,0:T(8,128)(2,1)S(1)}, u32[]{:S(2)}, u32[]{:S(2)}) collective-permute-start(bf16[64,2048]{1,0:T(8,128)(2,1)} %fusion.15), channel_id=1, source_target_pairs={{0,8},{8,0},{1,9},{9,1},{2,10},{10,2},{3,11},{11,3},{4,12},{12,4},... | collective-permute-start | bytes 786440 | tf_op jit(solution)/shard_map/ppermute | solution.py:121
  113.8 0.7 copy-start.12
  116.0 6.3 %collective-permute-start.20 = (f32[1,128]{1,0:T(1,128)S(1)}, f32[1,128]{1,0:T(1,128)S(1)}, u32[]{:S(2)}, u32[]{:S(2)}) collective-permute-start(f32[1,128]{1,0:T(1,128)S(1)} %maximum_bitcast_fusion.1), channel_id=1, source_target_pairs={{0,16},{16,0},{32,48},{48,32},{1,17},{17,1},{33,49},{49,33},{2,18}... | collective-permute-start | bytes 1544 | tf_op jit(solution)/shard_map/ppermute | solution.py:130
  122.4 15.1 %collective-permute-start.21 = (f32[1,128]{1,0:T(1,128)S(1)}, f32[1,128]{1,0:T(1,128)S(1)}, u32[]{:S(2)}, u32[]{:S(2)}) collective-permute-start(f32[1,128]{1,0:T(1,128)S(1)} %fusion.19), channel_id=1, source_target_pairs={{0,32},{16,48},{32,0},{48,16},{1,33},{17,49},{33,1},{49,17},{2,34}... | collective-permute-start | bytes 1544 | tf_op jit(solution)/shard_map/ppermute | solution.py:131
  127.8 10.8 %collective-permute-start.22 = (bf16[64,2048]{1,0:T(8,128)(2,1)S(1)}, bf16[64,2048]{1,0:T(8,128)(2,1)S(1)}, u32[]{:S(2)}, u32[]{:S(2)}) collective-permute-start(bf16[64,2048]{1,0:T(8,128)(2,1)S(1)} %get-tuple-element.34), channel_id=1, source_target_pairs={{0,64},{64,128},{128,192},{192,256},{256,320},{320,384},{384,448},... | collective-permute-start | bytes 786440 | tf_op jit(solution)/shard_map/ppermute | solution.py:126
  133.3 8.3 %collective-permute-start.23 = (bf16[64,2048]{1,0:T(8,128)(2,1)S(1)}, bf16[64,2048]{1,0:T(8,128)(2,1)S(1)}, u32[]{:S(2)}, u32[]{:S(2)}) collective-permute-start(bf16[64,2048]{1,0:T(8,128)(2,1)S(1)} %get-tuple-element.42), channel_id=1, source_target_pairs={{0,64},{64,128},{128,192},{192,256},{256,320},{320,384},{384,448},... | collective-permute-start | bytes 786440 | tf_op jit(solution)/shard_map/ppermute | solution.py:126

commit v2 on v0

v2 whole, which is shorter than its diff:
```python
import functools

import jax
import jax.numpy as jnp
from jax import lax
from jax.experimental import pallas as pl
from jax.experimental.pallas import tpu as pltpu
from jax.sharding import Mesh, PartitionSpec as P

WIDE = 512
PARTS = 4


def project(*refs, places, first_rel, added):
    n = len(places)
    sources, weights = refs[:n], refs[n:n + 2]
    before = refs[n + 2] if added else None
    out, rows, held, base, result, in_sem, out_sem = refs[-7:]
    d, me = lax.axis_index("dp"), lax.axis_index("tensor") % 4
    k, columns = weights[0].shape
    copies = []

    def fetch(source, target):
        copies.append(pltpu.make_async_copy(source, target, in_sem.at[len(copies)]))
        copies[-1].start()

    for source, (shift, begin) in zip(sources, places):
        slot = lax.rem(d + shift, PARTS)
        for i in range(2):
            fetch(source.at[me ^ (first_rel + i)], rows.at[slot, pl.ds(begin, source.shape[1]), pl.ds(i * k, k)])
    first = len(copies)
    each = 3 if added else 2
    for at in range(0, columns, WIDE):
        for i, weight in enumerate(weights):
            fetch(weight.at[:, pl.ds(at, WIDE)], held.at[pl.ds(i * k, k), pl.ds(at, WIDE)])
        if added:
            fetch(before.at[:, :, pl.ds(at, WIDE)], base.at[:, :, pl.ds(at, WIDE)])
    for copy in copies[:first]:
        copy.wait()
    lhs = rows[...].reshape(-1, 2 * k)
    sent = []
    for j, at in enumerate(range(0, columns, WIDE)):
        for copy in copies[first + each * j:first + each * (j + 1)]:
            copy.wait()
        value = jnp.dot(lhs, held[:, at:at + WIDE], preferred_element_type=jnp.float32).reshape(PARTS, -1, WIDE)
        if added:
            value += base[:, :, at:at + WIDE]
        result[:, :, at:at + WIDE] = value.astype(result.dtype)
        sent.append(pltpu.make_async_copy(result.at[:, :, pl.ds(at, WIDE)], out.at[:, :, pl.ds(at, WIDE)], out_sem.at[j]))
        sent[-1].start()
    for copy in sent:
        copy.wait()


def projected(places, first_rel, sources, weights, before, rows):
    k, columns = weights[0].shape
    tiles = columns // WIDE
    added = before is not None
    kind = jnp.bfloat16 if added else jnp.float32
    anywhere = pl.BlockSpec(memory_space=pl.ANY)
    operands = [*sources, *weights] + ([before] if added else [])
    return pl.pallas_call(
        functools.partial(project, places=places, first_rel=first_rel, added=added),
        in_specs=[anywhere] * len(operands),
        out_specs=anywhere,
        out_shape=jax.ShapeDtypeStruct((PARTS, rows, columns), kind),
        scratch_shapes=[
            pltpu.VMEM((PARTS, rows, 2 * k), jnp.bfloat16),
            pltpu.VMEM((2 * k, columns), jnp.bfloat16),
            pltpu.VMEM((PARTS, rows, columns) if added else (1, 8, 128), jnp.float32),
            pltpu.VMEM((PARTS, rows, columns), kind),
            pltpu.SemaphoreType.DMA((2 * len(sources) + 3 * tiles,)),
            pltpu.SemaphoreType.DMA((tiles,)),
        ],
        cost_estimate=pl.CostEstimate(
            flops=2 * PARTS * rows * 2 * k * columns,
            bytes_accessed=2 * (PARTS * rows * 2 * k + 2 * k * columns + 3 * PARTS * rows * columns),
            transcendentals=0),
        compiler_params=pltpu.CompilerParams(vmem_limit_bytes=24 * 2**20),
    )(*operands)


def after(value, *others):
    return lax.optimization_barrier((value, *others))[0]


def on_device(sections, context, residual, out_weight, norm_gain, valid_tokens):
    d = lax.axis_index("dp")
    t = lax.axis_index("tensor")
    width = context.shape[2]
    rows = residual.shape[1]
    r = rows // 2
    swap = [(i, i ^ 1) for i in range(16)]
    pair = [(i, i ^ 2) for i in range(16)]
    up = [(i, (i + 1) % 4) for i in range(4)]
    down = [(i, (i - 1) % 4) for i in range(4)]
    quads = [[4 * g + i for i in range(4)] for g in range(4)]
    across = [[4 * g + i for g in range(4)] for i in range(4)]

    tokens = lax.all_to_all(context.reshape(4, rows, width), "tensor", 0, 0, axis_index_groups=quads, tiled=True)
    weight = out_weight[0]
    near = [lax.ppermute(after(weight, tokens), "tensor", pair)]

    own_a, own_b = tokens[:, :r], tokens[:, r:]
    right_a = lax.ppermute(own_a, "dp", up)
    left_b = lax.ppermute(own_b, "dp", down)
    left_a = lax.ppermute(own_a, "dp", down)
    right_b = lax.ppermute(own_b, "dp", up)
    far_a = lax.ppermute(right_a, "dp", up)
    far_b = lax.ppermute(left_b, "dp", down)
    sources = [tokens, right_a, right_b, left_a, left_b, far_a, far_b]
    places = [(0, 0), (3, 0), (3, r), (1, 0), (1, r), (2, 0), (2, r)]
    w_core = lax.ppermute(weight, "tensor", swap)
    cross = [lax.ppermute(after(w, *sources), "tensor", swap) for w in near]

    part = projected(tuple(places), 0, sources, [weight, w_core], None, rows)
    part = projected(tuple(places), 2, sources, [*near, *cross], part, rows)
    got = lax.all_to_all(part, "tensor", 0, 0, axis_index_groups=across, tiled=True)
    h = residual[0].astype(jnp.float32) + jnp.sum(got.astype(jnp.float32), axis=0)
    row = t * rows + jnp.arange(rows, dtype=jnp.int32)
    live = (row < valid_tokens[0])[:, None]
    kept = jnp.where(live, h, 0.0)
    moved = lax.ppermute(kept.astype(jnp.bfloat16), "section", [(s, s + 1) for s in range(sections - 1)])
    square = jnp.sum(h * h, axis=1)[None]
    square = jnp.broadcast_to(square[None], (4, 1, rows))
    square = jnp.sum(lax.all_to_all(square, "dp", 0, 0, tiled=True), axis=0)
    scale = lax.rsqrt(square[0] / 8192.0 + 1e-06)
    gain = lax.dynamic_slice_in_dim(norm_gain[0], d * residual.shape[2], residual.shape[2])
    kept = after(kept, moved)
    normed = (kept * scale[:, None] * gain[None, :]).astype(jnp.bfloat16)
    return normed[None], moved[None]


def solution(mesh):
    placed = (
        P("section", "dp", "tensor"),
        P("section", "tensor", "dp"),
        P("section", "tensor", "dp"),
        P("section", None),
        P("section"),
    )
    return jax.shard_map(
        functools.partial(on_device, mesh.devices.shape[0]),
        mesh=mesh,
        in_specs=placed,
        out_specs=(P("section", "tensor", "dp"), P("section", "tensor", "dp")),
        check_vma=False,
    )
```

time: 216 us -> 132 us (0.61)
  the two profiles are of different devices: /device:TPU:71 before, /device:TPU:72 now
where the time goes in v2:
time: 132 us; the launch traced here: 131 us
  waiting for transfers between devices  56.2 us (43%)
  starting transfers between devices  46.1 us (35%)
  blocking collectives  12.4 us (9%)
  Pallas kernels  11.6 us (9%)
  other arithmetic  1.64 us (1%)
  between operations  1.53 us (1%)
  local copies, waits for them, and re-layouts  1.43 us (1%)
    all_to_all x1, waiting for transfers between devices, on_device(): lax.all_to_all(part, 'tensor', 0, 0, axis_index_groups=across, tiled=True)  25.7 us
    all_to_all x1, blocking collectives, on_device(): lax.all_to_all(context.reshape(4, rows, width), 'tensor', 0, 0, axis_inde...  12.4 us
    pallas_call x2, Pallas kernels, projected(): pl.pallas_call(functools.partial(project, places=places, first_rel=first_...  11.6 us
    all_to_all x1, waiting for transfers between devices, on_device(): square = jnp.sum(lax.all_to_all(square, 'dp', 0, 0, tiled=True), axis=0)  7.58 us
    all_to_all x1, starting transfers between devices, on_device(): square = jnp.sum(lax.all_to_all(square, 'dp', 0, 0, tiled=True), axis=0)  6.2 us
    ppermute x1, waiting for transfers between devices, on_device(): right_a = lax.ppermute(own_a, 'dp', up)  5.85 us
    all_to_all x1, starting transfers between devices, on_device(): lax.all_to_all(part, 'tensor', 0, 0, axis_index_groups=across, tiled=True)  5.76 us
    ppermute x1, starting transfers between devices, on_device(): left_a = lax.ppermute(own_a, 'dp', down)  4.67 us
  transfers between devices with their start and end apart: 12, of which 8 were waited for; matrix products, arithmetic and copies ran while one was open for 0% of the time, Pallas kernels for 4%

profile of v2, /device:TPU:72, one launch (start us, length us, event | category | flops | bytes accessed | tf_op | source)
XLA Modules:
  0.0 131.0 jit_solution(10863679406053064875)
XLA Ops:
  0.6 0.0 copy-start
  0.6 0.0 copy-start.1
  0.7 12.4 %all_to_all.15.refs_0_ = bf16[4,128,512]{2,1,0:T(8,128)(2,1)S(1)} all-to-all(bf16[4,128,512]{2,1,0:T(8,128)(2,1)} %bitcast.17), channel_id=1, replica_groups={{0,1,2,3},{4,5,6,7},{8,9,10,11},{12,13,14,15},{16,17,18,19},{20,21,22,2..., dimensions={0} | all-to-all | bytes 1048576 | tf_op jit(solution)/shard_map/all_to_all | solution.py:100
  13.1 2.3 %collective-permute-start.6 = (bf16[512,2048]{1,0:T(8,128)(2,1)}, bf16[512,2048]{1,0:T(8,128)(2,1)S(1)}, u32[]{:S(2)}, u32[]{:S(2)}) collective-permute-start(bf16[512,2048]{1,0:T(8,128)(2,1)} %bitcast.14), channel_id=1, source_target_pairs={{0,2},{1,3},{2,0},{3,1},{4,6},{5,7},{6,4},{7,5},{8,10},{9,11},{10,... | collective-permute-start | bytes 6291464 | tf_op jit(solution)/shard_map/ppermute | solution.py:102
  15.4 4.5 %collective-permute-start = (bf16[4,64,512]{2,1,0:T(8,128)(2,1)S(1)}, bf16[4,64,512]{2,1,0:T(8,128)(2,1)S(1)}, u32[]{:S(2)}, u32[]{:S(2)}) collective-permute-start(bf16[4,64,512]{2,1,0:T(8,128)(2,1)S(1)} %get-tuple-element.12), channel_id=1, source_target_pairs={{0,16},{16,32},{32,48},{48,0},{1,17},{17,33},{33,49},{49,1},{2,18}... | collective-permute-start | bytes 786440 | tf_op jit(solution)/shard_map/ppermute | solution.py:105
  19.9 3.5 %collective-permute-start.3 = (bf16[4,64,512]{2,1,0:T(8,128)(2,1)S(1)}, bf16[4,64,512]{2,1,0:T(8,128)(2,1)S(1)}, u32[]{:S(2)}, u32[]{:S(2)}) collective-permute-start(bf16[4,64,512]{2,1,0:T(8,128)(2,1)S(1)} %get-tuple-element.11), channel_id=1, source_target_pairs={{0,48},{16,0},{32,16},{48,32},{1,49},{17,1},{33,17},{49,33},{2,50}... | collective-permute-start | bytes 786440 | tf_op jit(solution)/shard_map/ppermute | solution.py:106
  23.4 3.3 %collective-permute-start.1 = (bf16[4,64,512]{2,1,0:T(8,128)(2,1)S(1)}, bf16[4,64,512]{2,1,0:T(8,128)(2,1)S(1)}, u32[]{:S(2)}, u32[]{:S(2)}) collective-permute-start(bf16[4,64,512]{2,1,0:T(8,128)(2,1)S(1)} %get-tuple-element.11), channel_id=1, source_target_pairs={{0,16},{16,32},{32,48},{48,0},{1,17},{17,33},{33,49},{49,1},{2,18}... | collective-permute-start | bytes 786440 | tf_op jit(solution)/shard_map/ppermute | solution.py:108
  26.7 4.7 %collective-permute-start.2 = (bf16[4,64,512]{2,1,0:T(8,128)(2,1)S(1)}, bf16[4,64,512]{2,1,0:T(8,128)(2,1)S(1)}, u32[]{:S(2)}, u32[]{:S(2)}) collective-permute-start(bf16[4,64,512]{2,1,0:T(8,128)(2,1)S(1)} %get-tuple-element.12), channel_id=1, source_target_pairs={{0,48},{16,0},{32,16},{48,32},{1,49},{17,1},{33,17},{49,33},{2,50}... | collective-permute-start | bytes 786440 | tf_op jit(solution)/shard_map/ppermute | solution.py:107
  31.3 5.8 %collective-permute-done.refs_1_ = bf16[4,64,512]{2,1,0:T(8,128)(2,1)S(1)} collective-permute-done((bf16[4,64,512]{2,1,0:T(8,128)(2,1)S(1)}, bf16[4,64,512]{2,1,0:T(8,128)(2,1)S(1)}, u32[]{:S(2)}, u32[]{:S(2)}) %collective-permute-start) | collective-permute-done | bytes 262176 | tf_op jit(solution)/shard_map/ppermute | solution.py:105
  37.2 4.1 %collective-permute-start.4 = (bf16[4,64,512]{2,1,0:T(8,128)(2,1)S(1)}, bf16[4,64,512]{2,1,0:T(8,128)(2,1)S(1)}, u32[]{:S(2)}, u32[]{:S(2)}) collective-permute-start(bf16[4,64,512]{2,1,0:T(8,128)(2,1)S(1)} %collective-permute-done.refs_1_), channel_id=1, source_target_pairs={{0,16},{16,32},{32,48},{48,0},{1,17},{17,33},{33,49},{49,1},{2,18}... | collective-permute-start | bytes 786440 | tf_op jit(solution)/shard_map/ppermute | solution.py:109
  41.3 0.0 collective-permute-done.3.refs_4_
  41.3 3.8 %collective-permute-start.5 = (bf16[4,64,512]{2,1,0:T(8,128)(2,1)S(1)}, bf16[4,64,512]{2,1,0:T(8,128)(2,1)S(1)}, u32[]{:S(2)}, u32[]{:S(2)}) collective-permute-start(bf16[4,64,512]{2,1,0:T(8,128)(2,1)S(1)} %collective-permute-done.3.refs_4_), channel_id=1, source_target_pairs={{0,48},{16,0},{32,16},{48,32},{1,49},{17,1},{33,17},{49,33},{2,50}... | collective-permute-start | bytes 786440 | tf_op jit(solution)/shard_map/ppermute | solution.py:110
  45.1 4.6 %collective-permute-done.1.refs_2_ = bf16[4,64,512]{2,1,0:T(8,128)(2,1)S(1)} collective-permute-done((bf16[4,64,512]{2,1,0:T(8,128)(2,1)S(1)}, bf16[4,64,512]{2,1,0:T(8,128)(2,1)S(1)}, u32[]{:S(2)}, u32[]{:S(2)}) %collective-permute-start.1) | collective-permute-done | bytes 262176 | tf_op jit(solution)/shard_map/ppermute | solution.py:108
  49.8 0.0 copy-done.1
  49.8 1.9 %collective-permute-start.8 = (bf16[512,2048]{1,0:T(8,128)(2,1)S(1)}, bf16[512,2048]{1,0:T(8,128)(2,1)S(1)}, u32[]{:S(2)}, u32[]{:S(2)}) collective-permute-start(bf16[512,2048]{1,0:T(8,128)(2,1)S(1)} %bitcast.15), channel_id=1, source_target_pairs={{0,1},{1,0},{2,3},{3,2},{4,5},{5,4},{6,7},{7,6},{8,9},{9,8},{10,11... | collective-permute-start | bytes 6291464 | tf_op jit(solution)/shard_map/ppermute | solution.py:113
  51.7 0.0 collective-permute-done.2.refs_3_
  51.7 3.6 %collective-permute-done.4.refs_5_ = bf16[4,64,512]{2,1,0:T(8,128)(2,1)S(1)} collective-permute-done((bf16[4,64,512]{2,1,0:T(8,128)(2,1)S(1)}, bf16[4,64,512]{2,1,0:T(8,128)(2,1)S(1)}, u32[]{:S(2)}, u32[]{:S(2)}) %collective-permute-start.4) | collective-permute-done | bytes 262176 | tf_op jit(solution)/shard_map/ppermute | solution.py:109
  55.3 2.7 %collective-permute-done.5.refs_6_ = bf16[4,64,512]{2,1,0:T(8,128)(2,1)S(1)} collective-permute-done((bf16[4,64,512]{2,1,0:T(8,128)(2,1)S(1)}, bf16[4,64,512]{2,1,0:T(8,128)(2,1)S(1)}, u32[]{:S(2)}, u32[]{:S(2)}) %collective-permute-start.5) | collective-permute-done | bytes 262176 | tf_op jit(solution)/shard_map/ppermute | solution.py:110
  58.0 4.2 %collective-permute-done.6.refs_7_ = bf16[512,2048]{1,0:T(8,128)(2,1)S(1)} collective-permute-done((bf16[512,2048]{1,0:T(8,128)(2,1)}, bf16[512,2048]{1,0:T(8,128)(2,1)S(1)}, u32[]{:S(2)}, u32[]{:S(2)}) %collective-permute-start.6) | collective-permute-done | bytes 2097184 | tf_op jit(solution)/shard_map/ppermute | solution.py:102
  62.2 1.9 %collective-permute-start.7 = (bf16[512,2048]{1,0:T(8,128)(2,1)S(1)}, bf16[512,2048]{1,0:T(8,128)(2,1)S(1)}, u32[]{:S(2)}, u32[]{:S(2)}) collective-permute-start(bf16[512,2048]{1,0:T(8,128)(2,1)S(1)} %collective-permute-done.6.refs_7_), channel_id=1, source_target_pairs={{0,1},{1,0},{2,3},{3,2},{4,5},{5,4},{6,7},{7,6},{8,9},{9,8},{10,11... | collective-permute-start | bytes 6291464 | tf_op jit(solution)/shard_map/ppermute | solution.py:114
  64.1 0.0 collective-permute-done.8.refs_8_
  64.1 5.4 %shard_map.68.refs_9_ = f32[4,128,2048]{2,1,0:T(8,128)S(1)} custom-call(bf16[4,128,512]{2,1,0:T(8,128)(2,1)S(1)} %all_to_all.15.refs_0_, bf16[4,64,512]{2,1,0:T(8,128)(2,1)S(1)} %collective-permute-done.refs_1_, bf16[4,64,512]{2,1,0:T(8,128)(2,1)S(1)} %collective-permute-done.1.refs_2_, bf16[4,64,512]{2,1,0:T(8,128)(2,1)S(1)} %collective-permute-done.2.refs_3_, ...), custom_call_target="tpu_custom_call" | custom-call | flops 2147483648 | bytes 11534336 | tf_op jit(solution)/shard_map/pallas_call | solution.py:62
  69.5 0.0 collective-permute-done.7.refs_8_
  69.5 6.2 %shard_map.69 = bf16[4,128,2048]{2,1,0:T(8,128)(2,1)} custom-call(bf16[4,128,512]{2,1,0:T(8,128)(2,1)S(1)} %all_to_all.15.refs_0_, bf16[4,64,512]{2,1,0:T(8,128)(2,1)S(1)} %collective-permute-done.refs_1_, bf16[4,64,512]{2,1,0:T(8,128)(2,1)S(1)} %collective-permute-done.1.refs_2_, bf16[4,64,512]{2,1,0:T(8,128)(2,1)S(1)} %collective-permute-done.2.refs_3_, ...), custom_call_target="tpu_custom_call" | custom-call | flops 2147483648 | bytes 11534336 | tf_op jit(solution)/shard_map/pallas_call | solution.py:62
  75.8 5.8 %all-to-all-start.1 = ((bf16[4,128,2048]{2,1,0:T(8,128)(2,1)}), bf16[4,128,2048]{2,1,0:T(8,128)(2,1)S(1)}, u32[]{:S(2)}, u32[]{:S(2)}) async-start(bf16[4,128,2048]{2,1,0:T(8,128)(2,1)} %shard_map.69), calls=%async_computation.1 | async-start | bytes 4194304 | tf_op jit(solution)/shard_map/all_to_all | solution.py:118
  81.5 0.0 copy-start.2
  82.3 25.7 %all-to-all-done.1 = bf16[4,128,2048]{2,1,0:T(8,128)(2,1)S(1)} async-done(((bf16[4,128,2048]{2,1,0:T(8,128)(2,1)}), bf16[4,128,2048]{2,1,0:T(8,128)(2,1)S(1)}, u32[]{:S(2)}, u32[]{:S(2)}) %all-to-all-start.1) | async-done | bytes 2097184 | tf_op jit(solution)/shard_map/all_to_all | solution.py:118
  108.0 0.4 convert_reduce_fusion
  108.4 0.0 copy-done.2
  108.4 0.3 fusion.2
  108.6 4.3 %collective-permute-start.9 = (bf16[128,2048]{1,0:T(8,128)(2,1)S(1)}, bf16[128,2048]{1,0:T(8,128)(2,1)S(1)}, u32[]{:S(2)}, u32[]{:S(2)}) collective-permute-start(bf16[128,2048]{1,0:T(8,128)(2,1)S(1)} %get-tuple-element.8), channel_id=1, source_target_pairs={{0,64},{64,128},{128,192},{192,256},{256,320},{320,384},{384,448},... | collective-permute-start | bytes 1572872 | tf_op jit(solution)/shard_map/ppermute | solution.py:123
  112.9 0.6 broadcast_in_dim.28
  113.5 6.2 %all-to-all-start.2 = ((f32[4,1,128]{2,1,0:T(1,128)}), f32[4,1,128]{2,1,0:T(1,128)S(1)}, u32[]{:S(2)}, u32[]{:S(2)}) async-start(f32[4,1,128]{2,1,0:T(1,128)} %broadcast_in_dim.28), calls=%async_computation.2 | async-start | bytes 4096 | tf_op jit(solution)/shard_map/all_to_all | solution.py:126
  119.7 0.0 copy-done
  119.7 7.6 %all-to-all-done.2 = f32[4,1,128]{2,1,0:T(1,128)S(1)} async-done(((f32[4,1,128]{2,1,0:T(1,128)}), f32[4,1,128]{2,1,0:T(1,128)S(1)}, u32[]{:S(2)}, u32[]{:S(2)}) %all-to-all-start.2) | async-done | bytes 2080 | tf_op jit(solution)/shard_map/all_to_all | solution.py:126
  127.3 2.0 %collective-permute-done.9 = bf16[128,2048]{1,0:T(8,128)(2,1)S(1)} collective-permute-done((bf16[128,2048]{1,0:T(8,128)(2,1)S(1)}, bf16[128,2048]{1,0:T(8,128)(2,1)S(1)}, u32[]{:S(2)}, u32[]{:S(2)}) %collective-permute-start.9) | collective-permute-done | bytes 524320 | tf_op jit(solution)/shard_map/ppermute | solution.py:123
  129.3 0.9 fusion.1
  130.2 0.8 copy.10
  (5 shorter events, 0.1 us)
Async XLA Ops:
  0.6 119.1 %copy-start = (f32[1,8192]{1,0:T(1,128)S(1)}, f32[1,8192]{1,0:T(1,128)}, u32[]{:S(2)}) copy-start(f32[1,8192]{1,0:T(1,128)} %param.8) | copy-start | bytes 98308
  0.6 49.1 %copy-start.1 = (bf16[1,512,2048]{2,1,0:T(8,128)(2,1)S(1)}, bf16[1,512,2048]{2,1,0:T(8,128)(2,1)}, u32[]{:S(2)}) copy-start(bf16[1,512,2048]{2,1,0:T(8,128)(2,1)} %param.7) | copy-start | bytes 6291460
  13.1 49.1 %collective-permute-start.6 = (bf16[512,2048]{1,0:T(8,128)(2,1)}, bf16[512,2048]{1,0:T(8,128)(2,1)S(1)}, u32[]{:S(2)}, u32[]{:S(2)}) collective-permute-start(bf16[512,2048]{1,0:T(8,128)(2,1)} %bitcast.14), channel_id=1, source_target_pairs={{0,2},{1,3},{2,0},{3,1},{4,6},{5,7},{6,4},{7,5},{8,10},{9,11},{10,... | collective-permute-start | bytes 6291464 | tf_op jit(solution)/shard_map/ppermute | solution.py:102
  15.4 21.8 %collective-permute-start = (bf16[4,64,512]{2,1,0:T(8,128)(2,1)S(1)}, bf16[4,64,512]{2,1,0:T(8,128)(2,1)S(1)}, u32[]{:S(2)}, u32[]{:S(2)}) collective-permute-start(bf16[4,64,512]{2,1,0:T(8,128)(2,1)S(1)} %get-tuple-element.12), channel_id=1, source_target_pairs={{0,16},{16,32},{32,48},{48,0},{1,17},{17,33},{33,49},{49,1},{2,18}... | collective-permute-start | bytes 786440 | tf_op jit(solution)/shard_map/ppermute | solution.py:105
  19.9 21.4 %collective-permute-start.3 = (bf16[4,64,512]{2,1,0:T(8,128)(2,1)S(1)}, bf16[4,64,512]{2,1,0:T(8,128)(2,1)S(1)}, u32[]{:S(2)}, u32[]{:S(2)}) collective-permute-start(bf16[4,64,512]{2,1,0:T(8,128)(2,1)S(1)} %get-tuple-element.11), channel_id=1, source_target_pairs={{0,48},{16,0},{32,16},{48,32},{1,49},{17,1},{33,17},{49,33},{2,50}... | collective-permute-start | bytes 786440 | tf_op jit(solution)/shard_map/ppermute | solution.py:106
  23.4 26.4 %collective-permute-start.1 = (bf16[4,64,512]{2,1,0:T(8,128)(2,1)S(1)}, bf16[4,64,512]{2,1,0:T(8,128)(2,1)S(1)}, u32[]{:S(2)}, u32[]{:S(2)}) collective-permute-start(bf16[4,64,512]{2,1,0:T(8,128)(2,1)S(1)} %get-tuple-element.11), channel_id=1, source_target_pairs={{0,16},{16,32},{32,48},{48,0},{1,17},{17,33},{33,49},{49,1},{2,18}... | collective-permute-start | bytes 786440 | tf_op jit(solution)/shard_map/ppermute | solution.py:108
  26.7 25.0 %collective-permute-start.2 = (bf16[4,64,512]{2,1,0:T(8,128)(2,1)S(1)}, bf16[4,64,512]{2,1,0:T(8,128)(2,1)S(1)}, u32[]{:S(2)}, u32[]{:S(2)}) collective-permute-start(bf16[4,64,512]{2,1,0:T(8,128)(2,1)S(1)} %get-tuple-element.12), channel_id=1, source_target_pairs={{0,48},{16,0},{32,16},{48,32},{1,49},{17,1},{33,17},{49,33},{2,50}... | collective-permute-start | bytes 786440 | tf_op jit(solution)/shard_map/ppermute | solution.py:107
  37.2 18.1 %collective-permute-start.4 = (bf16[4,64,512]{2,1,0:T(8,128)(2,1)S(1)}, bf16[4,64,512]{2,1,0:T(8,128)(2,1)S(1)}, u32[]{:S(2)}, u32[]{:S(2)}) collective-permute-start(bf16[4,64,512]{2,1,0:T(8,128)(2,1)S(1)} %collective-permute-done.refs_1_), channel_id=1, source_target_pairs={{0,16},{16,32},{32,48},{48,0},{1,17},{17,33},{33,49},{49,1},{2,18}... | collective-permute-start | bytes 786440 | tf_op jit(solution)/shard_map/ppermute | solution.py:109
  41.3 16.6 %collective-permute-start.5 = (bf16[4,64,512]{2,1,0:T(8,128)(2,1)S(1)}, bf16[4,64,512]{2,1,0:T(8,128)(2,1)S(1)}, u32[]{:S(2)}, u32[]{:S(2)}) collective-permute-start(bf16[4,64,512]{2,1,0:T(8,128)(2,1)S(1)} %collective-permute-done.3.refs_4_), channel_id=1, source_target_pairs={{0,48},{16,0},{32,16},{48,32},{1,49},{17,1},{33,17},{49,33},{2,50}... | collective-permute-start | bytes 786440 | tf_op jit(solution)/shard_map/ppermute | solution.py:110
  49.8 14.3 %collective-permute-start.8 = (bf16[512,2048]{1,0:T(8,128)(2,1)S(1)}, bf16[512,2048]{1,0:T(8,128)(2,1)S(1)}, u32[]{:S(2)}, u32[]{:S(2)}) collective-permute-start(bf16[512,2048]{1,0:T(8,128)(2,1)S(1)} %bitcast.15), channel_id=1, source_target_pairs={{0,1},{1,0},{2,3},{3,2},{4,5},{5,4},{6,7},{7,6},{8,9},{9,8},{10,11... | collective-permute-start | bytes 6291464 | tf_op jit(solution)/shard_map/ppermute | solution.py:113
  62.2 7.3 %collective-permute-start.7 = (bf16[512,2048]{1,0:T(8,128)(2,1)S(1)}, bf16[512,2048]{1,0:T(8,128)(2,1)S(1)}, u32[]{:S(2)}, u32[]{:S(2)}) collective-permute-start(bf16[512,2048]{1,0:T(8,128)(2,1)S(1)} %collective-permute-done.6.refs_7_), channel_id=1, source_target_pairs={{0,1},{1,0},{2,3},{3,2},{4,5},{5,4},{6,7},{7,6},{8,9},{9,8},{10,11... | collective-permute-start | bytes 6291464 | tf_op jit(solution)/shard_map/ppermute | solution.py:114
  75.8 32.2 %all-to-all-start.1 = ((bf16[4,128,2048]{2,1,0:T(8,128)(2,1)}), bf16[4,128,2048]{2,1,0:T(8,128)(2,1)S(1)}, u32[]{:S(2)}, u32[]{:S(2)}) async-start(bf16[4,128,2048]{2,1,0:T(8,128)(2,1)} %shard_map.69), calls=%async_computation.1 | async-start | bytes 4194304 | tf_op jit(solution)/shard_map/all_to_all | solution.py:118
  81.5 26.8 %copy-start.2 = (bf16[1,128,2048]{2,1,0:T(8,128)(2,1)S(1)}, bf16[1,128,2048]{2,1,0:T(8,128)(2,1)}, u32[]{:S(2)}) copy-start(bf16[1,128,2048]{2,1,0:T(8,128)(2,1)} %param.6) | copy-start | bytes 1572868
  108.6 20.6 %collective-permute-start.9 = (bf16[128,2048]{1,0:T(8,128)(2,1)S(1)}, bf16[128,2048]{1,0:T(8,128)(2,1)S(1)}, u32[]{:S(2)}, u32[]{:S(2)}) collective-permute-start(bf16[128,2048]{1,0:T(8,128)(2,1)S(1)} %get-tuple-element.8), channel_id=1, source_target_pairs={{0,64},{64,128},{128,192},{192,256},{256,320},{320,384},{384,448},... | collective-permute-start | bytes 1572872 | tf_op jit(solution)/shard_map/ppermute | solution.py:123
  113.5 13.8 %all-to-all-start.2 = ((f32[4,1,128]{2,1,0:T(1,128)}), f32[4,1,128]{2,1,0:T(1,128)S(1)}, u32[]{:S(2)}, u32[]{:S(2)}) async-start(f32[4,1,128]{2,1,0:T(1,128)} %broadcast_in_dim.28), calls=%async_computation.2 | async-start | bytes 4096 | tf_op jit(solution)/shard_map/all_to_all | solution.py:126

commit v3 on v2

v3 whole, which is shorter than its diff:
```python
import functools

import jax
import jax.numpy as jnp
from jax import lax
from jax.experimental import pallas as pl
from jax.experimental.pallas import tpu as pltpu
from jax.sharding import Mesh, PartitionSpec as P

WIDE = 512
CUT = 1024
PARTS = 4


def project(*refs, places, first_rel, going):
    n = len(places)
    sources, weights = refs[:n], refs[n:n + 2]
    added = going is not None
    before = refs[n + 2] if added else None
    outs, (rows, held, base, result, in_sem, out_sem) = refs[n + 2 + added:-6], refs[-6:]
    d, t = lax.axis_index("dp"), lax.axis_index("tensor")
    ylo, xh, me = t // 8, (t // 4) % 2, t % 4
    k, columns = weights[0].shape
    copies = []

    def fetch(source, target):
        copies.append(pltpu.make_async_copy(source, target, in_sem.at[len(copies)]))
        copies[-1].start()

    for source, (shift, begin) in zip(sources, places):
        slot = lax.rem(d + shift, PARTS)
        order = me ^ (((slot % 2) ^ xh) * 2)
        for i in range(2):
            fetch(source.at[order ^ (first_rel + i)], rows.at[slot, pl.ds(begin, source.shape[1]), pl.ds(i * k, k)])
    first = len(copies)
    if going:
        wanted = ([(1 - ylo) * 2 + i for i in range(2)], [i * 2 + 1 - xh for i in range(2)])
    else:
        wanted = ([ylo * 2 + i for i in range(2)], [i * 2 + xh for i in range(2)])
    each = 4 if added else 2
    for at in range(0, columns, WIDE):
        for i, weight in enumerate(weights):
            fetch(weight.at[:, pl.ds(at, WIDE)], held.at[pl.ds(i * k, k), pl.ds(at, WIDE)])
        if added:
            for i, block in enumerate(wanted[at // CUT]):
                fetch(before.at[block, :, pl.ds(at, WIDE)], base.at[i, :, pl.ds(at, WIDE)])
    for copy in copies[:first]:
        copy.wait()
    sent = []
    for j, at in enumerate(range(0, columns, WIDE)):
        if not added:
            lhs = rows[...].reshape(-1, 2 * k)
        elif at % CUT == 0:
            lhs = jnp.concatenate([rows[block] for block in wanted[at // CUT]], axis=0)
        for copy in copies[first + each * j:first + each * (j + 1)]:
            copy.wait()
        value = jnp.dot(lhs, held[:, at:at + WIDE], preferred_element_type=jnp.float32).reshape(result.shape[0], -1, WIDE)
        if added:
            value += base[:, :, at:at + WIDE].astype(jnp.float32)
        result[:, :, at:at + WIDE] = value.astype(result.dtype)
        target, to = (outs[at // CUT], at % CUT) if added else (outs[0], at)
        sent.append(pltpu.make_async_copy(result.at[:, :, pl.ds(at, WIDE)], target.at[:, :, pl.ds(to, WIDE)], out_sem.at[j]))
        sent[-1].start()
    for copy in sent:
        copy.wait()


def projected(places, first_rel, sources, weights, before, rows, going=None):
    k, columns = weights[0].shape
    tiles = columns // WIDE
    added = going is not None
    parts = 2 if added else PARTS
    shapes = [(2, rows, CUT)] * 2 if added else [(PARTS, rows, columns)]
    anywhere = pl.BlockSpec(memory_space=pl.ANY)
    operands = [*sources, *weights] + ([before] if added else [])
    return pl.pallas_call(
        functools.partial(project, places=places, first_rel=first_rel, going=going),
        in_specs=[anywhere] * len(operands),
        out_specs=[anywhere] * len(shapes),
        out_shape=[jax.ShapeDtypeStruct(shape, jnp.bfloat16 if added else jnp.bfloat16) for shape in shapes],
        scratch_shapes=[
            pltpu.VMEM((PARTS, rows, 2 * k), jnp.bfloat16),
            pltpu.VMEM((2 * k, columns), jnp.bfloat16),
            pltpu.VMEM((2, rows, columns) if added else (1, 16, 128), jnp.bfloat16),
            pltpu.VMEM((parts, rows, columns), jnp.bfloat16 if added else jnp.bfloat16),
            pltpu.SemaphoreType.DMA((2 * len(sources) + 4 * tiles,)),
            pltpu.SemaphoreType.DMA((tiles,)),
        ],
        cost_estimate=pl.CostEstimate(
            flops=2 * parts * rows * 2 * k * columns,
            bytes_accessed=2 * (PARTS * rows * 2 * k + 2 * k * columns + 2 * parts * rows * columns),
            transcendentals=0),
        compiler_params=pltpu.CompilerParams(vmem_limit_bytes=24 * 2**20),
    )(*operands)


def split_sum(keep, got, mine, give, *, over):
    t = lax.axis_index("tensor")
    here = (t // 4) % 2 if over == "x" else t // 8
    mine[...] = keep[here].astype(jnp.float32) + got[here].astype(jnp.float32)
    give[...] = (keep[1 - here].astype(jnp.float32) + got[1 - here].astype(jnp.float32)).astype(jnp.bfloat16)


def split_summed(keep, got, over):
    _, n, m = keep.shape
    vmem = pl.BlockSpec(memory_space=pltpu.VMEM)
    return pl.pallas_call(
        functools.partial(split_sum, over=over),
        in_specs=[vmem] * 2,
        out_specs=[vmem] * 2,
        out_shape=[jax.ShapeDtypeStruct((n, m), kind) for kind in (jnp.float32, jnp.bfloat16)],
        cost_estimate=pl.CostEstimate(flops=2 * n * m, bytes_accessed=11 * n * m, transcendentals=0),
        compiler_params=pltpu.CompilerParams(vmem_limit_bytes=8 * 2**20),
    )(keep, got)


def after(value, *others):
    return lax.optimization_barrier((value, *others))[0]


def on_device(sections, context, residual, out_weight, norm_gain, valid_tokens):
    d = lax.axis_index("dp")
    t = lax.axis_index("tensor")
    width = context.shape[2]
    rows = residual.shape[1]
    r = rows // 2
    swap = [(i, i ^ 1) for i in range(16)]
    pair = [(i, i ^ 2) for i in range(16)]
    up = [(i, (i + 1) % 4) for i in range(4)]
    down = [(i, (i - 1) % 4) for i in range(4)]
    quads = [[16 * dd + 4 * g + (i ^ (2 * ((dd ^ g) % 2))) for i in range(4)] for dd in range(4) for g in range(4)]
    across = [[4 * g + i for g in range(4)] for i in range(4)]

    tokens = lax.all_to_all(context.reshape(4, rows, width), ("dp", "tensor"), 0, 0, axis_index_groups=quads, tiled=True)
    weight = out_weight[0]
    near = [lax.ppermute(after(weight, tokens), "tensor", pair)]

    own_a, own_b = tokens[:, :r], tokens[:, r:]
    right_a = lax.ppermute(own_a, "dp", up)
    left_b = lax.ppermute(own_b, "dp", down)
    left_a = lax.ppermute(own_a, "dp", down)
    right_b = lax.ppermute(own_b, "dp", up)
    far_a = lax.ppermute(right_a, "dp", up)
    far_b = lax.ppermute(left_b, "dp", down)
    sources = [tokens, right_a, right_b, left_a, left_b, far_a, far_b]
    places = [(0, 0), (3, 0), (3, r), (1, 0), (1, r), (2, 0), (2, r)]
    w_core = lax.ppermute(weight, "tensor", swap)
    cross = [lax.ppermute(after(w, *sources), "tensor", swap) for w in near]

    (part,) = projected(tuple(places), 0, sources, [weight, w_core], None, rows)
    send_a, send_b = projected(tuple(places), 2, sources, [*near, *cross], part, rows, True)
    keep_a, keep_b = projected(tuple(places), 2, sources, [*near, *cross], part, rows, False)
    over_y = [(i, i ^ 8) for i in range(16)]
    over_x = [(i, i ^ 6) for i in range(16)]
    got_b = lax.ppermute(send_b, "tensor", over_x)
    got_a = lax.ppermute(send_a, "tensor", over_y)
    keep_b, send_b = split_summed(keep_b, got_b, "y")
    keep_a, send_a = split_summed(keep_a, got_a, "x")
    got_a = lax.ppermute(send_a, "tensor", over_x)
    got_b = lax.ppermute(send_b, "tensor", over_y)
    attn = jnp.concatenate([keep_a + got_a.astype(jnp.float32), keep_b + got_b.astype(jnp.float32)], axis=1)
    h = residual[0].astype(jnp.float32) + attn
    row = t * rows + jnp.arange(rows, dtype=jnp.int32)
    live = (row < valid_tokens[0])[:, None]
    kept = jnp.where(live, h, 0.0)
    onward = [(s, s + 1) for s in range(sections - 1)]
    sending = kept.astype(jnp.bfloat16)
    square = jnp.sum(h * h, axis=1)[None]
    GATE = 0
    if GATE:
        begun = lax.ppermute(sending[:GATE], "section", onward)
        moved = jnp.concatenate([begun, lax.ppermute(sending[GATE:], "section", onward)])
        square = after(square, begun)
    else:
        moved = lax.ppermute(sending, "section", onward)
    square = lax.psum(square, "dp")
    scale = lax.rsqrt(square[0] / 8192.0 + 1e-06)
    gain = lax.dynamic_slice_in_dim(norm_gain[0], d * residual.shape[2], residual.shape[2])
    kept = after(kept, moved)
    normed = (kept * scale[:, None] * gain[None, :]).astype(jnp.bfloat16)
    return normed[None], moved[None]


def solution(mesh):
    placed = (
        P("section", "dp", "tensor"),
        P("section", "tensor", "dp"),
        P("section", "tensor", "dp"),
        P("section", None),
        P("section"),
    )
    return jax.shard_map(
        functools.partial(on_device, mesh.devices.shape[0]),
        mesh=mesh,
        in_specs=placed,
        out_specs=(P("section", "tensor", "dp"), P("section", "tensor", "dp")),
        check_vma=False,
    )
```

time: 132 us -> 126 us (0.955)
  the two profiles are of different devices: /device:TPU:72 before, /device:TPU:64 now
where the time goes in v3:
time: 126 us; the launch traced here: 125 us
  starting transfers between devices  51.2 us (41%)
  waiting for transfers between devices  32.5 us (26%)
  blocking collectives  24.9 us (20%)
  Pallas kernels  12.8 us (10%)
  between operations  1.55 us (1%)
  other arithmetic  1.35 us (1%)
    pallas_call x3, Pallas kernels, projected(): pl.pallas_call(functools.partial(project, places=places, first_rel=first_...  12.6 us
    psum x1, blocking collectives, on_device(): square = lax.psum(square, 'dp')  12.5 us
    all_to_all x1, blocking collectives, on_device(): lax.all_to_all(context.reshape(4, rows, width), ('dp', 'tensor'), 0, 0, a...  12.4 us
    ppermute x1, waiting for transfers between devices, on_device(): left_b = lax.ppermute(own_b, 'dp', down)  7.4 us
    ppermute x1, starting transfers between devices, on_device(): right_a = lax.ppermute(own_a, 'dp', up)  5.63 us
    ppermute x1, starting transfers between devices, on_device(): got_a = lax.ppermute(send_a, 'tensor', over_x)  4.8 us
    ppermute x1, starting transfers between devices, on_device(): left_a = lax.ppermute(own_a, 'dp', down)  4.8 us
    ppermute x1, starting transfers between devices, on_device(): far_b = lax.ppermute(left_b, 'dp', down)  4.79 us
  transfers between devices with their start and end apart: 14, of which 10 were waited for; matrix products, arithmetic and copies ran while one was open for 0% of the time, Pallas kernels for 7%

profile of v3, /device:TPU:64, one launch (start us, length us, event | category | flops | bytes accessed | tf_op | source)
XLA Modules:
  0.0 125.3 jit_solution(15002383612903731382)
XLA Ops:
  0.6 0.0 copy-start
  0.6 0.0 copy-start.1
  0.7 12.4 %all_to_all.5.refs_0_ = bf16[4,128,512]{2,1,0:T(8,128)(2,1)S(1)} all-to-all(bf16[4,128,512]{2,1,0:T(8,128)(2,1)} %bitcast.19), channel_id=1, replica_groups={{0,1,2,3},{6,7,4,5},{8,9,10,11},{14,15,12,13},{18,19,16,17},{20,21,22,2..., dimensions={0} | all-to-all | bytes 1048576 | tf_op jit(solution)/shard_map/all_to_all | solution.py:134
  13.1 2.3 %collective-permute-start.6 = (bf16[512,2048]{1,0:T(8,128)(2,1)}, bf16[512,2048]{1,0:T(8,128)(2,1)S(1)}, u32[]{:S(2)}, u32[]{:S(2)}) collective-permute-start(bf16[512,2048]{1,0:T(8,128)(2,1)} %bitcast.16), channel_id=1, source_target_pairs={{0,2},{1,3},{2,0},{3,1},{4,6},{5,7},{6,4},{7,5},{8,10},{9,11},{10,... | collective-permute-start | bytes 6291464 | tf_op jit(solution)/shard_map/ppermute | solution.py:136
  15.4 5.6 %collective-permute-start = (bf16[4,64,512]{2,1,0:T(8,128)(2,1)S(1)}, bf16[4,64,512]{2,1,0:T(8,128)(2,1)S(1)}, u32[]{:S(2)}, u32[]{:S(2)}) collective-permute-start(bf16[4,64,512]{2,1,0:T(8,128)(2,1)S(1)} %get-tuple-element.28), channel_id=1, source_target_pairs={{0,16},{16,32},{32,48},{48,0},{1,17},{17,33},{33,49},{49,1},{2,18}... | collective-permute-start | bytes 786440 | tf_op jit(solution)/shard_map/ppermute | solution.py:139
  21.0 3.6 %collective-permute-start.3 = (bf16[4,64,512]{2,1,0:T(8,128)(2,1)S(1)}, bf16[4,64,512]{2,1,0:T(8,128)(2,1)S(1)}, u32[]{:S(2)}, u32[]{:S(2)}) collective-permute-start(bf16[4,64,512]{2,1,0:T(8,128)(2,1)S(1)} %get-tuple-element.27), channel_id=1, source_target_pairs={{0,48},{16,0},{32,16},{48,32},{1,49},{17,1},{33,17},{49,33},{2,50}... | collective-permute-start | bytes 786440 | tf_op jit(solution)/shard_map/ppermute | solution.py:140
  24.6 3.2 %collective-permute-start.1 = (bf16[4,64,512]{2,1,0:T(8,128)(2,1)S(1)}, bf16[4,64,512]{2,1,0:T(8,128)(2,1)S(1)}, u32[]{:S(2)}, u32[]{:S(2)}) collective-permute-start(bf16[4,64,512]{2,1,0:T(8,128)(2,1)S(1)} %get-tuple-element.27), channel_id=1, source_target_pairs={{0,16},{16,32},{32,48},{48,0},{1,17},{17,33},{33,49},{49,1},{2,18}... | collective-permute-start | bytes 786440 | tf_op jit(solution)/shard_map/ppermute | solution.py:142
  27.8 4.8 %collective-permute-start.2 = (bf16[4,64,512]{2,1,0:T(8,128)(2,1)S(1)}, bf16[4,64,512]{2,1,0:T(8,128)(2,1)S(1)}, u32[]{:S(2)}, u32[]{:S(2)}) collective-permute-start(bf16[4,64,512]{2,1,0:T(8,128)(2,1)S(1)} %get-tuple-element.28), channel_id=1, source_target_pairs={{0,48},{16,0},{32,16},{48,32},{1,49},{17,1},{33,17},{49,33},{2,50}... | collective-permute-start | bytes 786440 | tf_op jit(solution)/shard_map/ppermute | solution.py:141
  32.6 3.6 %collective-permute-done.refs_1_ = bf16[4,64,512]{2,1,0:T(8,128)(2,1)S(1)} collective-permute-done((bf16[4,64,512]{2,1,0:T(8,128)(2,1)S(1)}, bf16[4,64,512]{2,1,0:T(8,128)(2,1)S(1)}, u32[]{:S(2)}, u32[]{:S(2)}) %collective-permute-start) | collective-permute-done | bytes 262176 | tf_op jit(solution)/shard_map/ppermute | solution.py:139
  36.2 2.5 %collective-permute-start.4 = (bf16[4,64,512]{2,1,0:T(8,128)(2,1)S(1)}, bf16[4,64,512]{2,1,0:T(8,128)(2,1)S(1)}, u32[]{:S(2)}, u32[]{:S(2)}) collective-permute-start(bf16[4,64,512]{2,1,0:T(8,128)(2,1)S(1)} %collective-permute-done.refs_1_), channel_id=1, source_target_pairs={{0,16},{16,32},{32,48},{48,0},{1,17},{17,33},{33,49},{49,1},{2,18}... | collective-permute-start | bytes 786440 | tf_op jit(solution)/shard_map/ppermute | solution.py:143
  38.7 7.4 %collective-permute-done.3.refs_4_ = bf16[4,64,512]{2,1,0:T(8,128)(2,1)S(1)} collective-permute-done((bf16[4,64,512]{2,1,0:T(8,128)(2,1)S(1)}, bf16[4,64,512]{2,1,0:T(8,128)(2,1)S(1)}, u32[]{:S(2)}, u32[]{:S(2)}) %collective-permute-start.3) | collective-permute-done | bytes 262176 | tf_op jit(solution)/shard_map/ppermute | solution.py:140
  46.1 4.8 %collective-permute-start.5 = (bf16[4,64,512]{2,1,0:T(8,128)(2,1)S(1)}, bf16[4,64,512]{2,1,0:T(8,128)(2,1)S(1)}, u32[]{:S(2)}, u32[]{:S(2)}) collective-permute-start(bf16[4,64,512]{2,1,0:T(8,128)(2,1)S(1)} %collective-permute-done.3.refs_4_), channel_id=1, source_target_pairs={{0,48},{16,0},{32,16},{48,32},{1,49},{17,1},{33,17},{49,33},{2,50}... | collective-permute-start | bytes 786440 | tf_op jit(solution)/shard_map/ppermute | solution.py:144
  50.9 0.0 collective-permute-done.1.refs_2_
  50.9 0.0 copy-done.1
  50.9 1.9 %collective-permute-start.8 = (bf16[512,2048]{1,0:T(8,128)(2,1)S(1)}, bf16[512,2048]{1,0:T(8,128)(2,1)S(1)}, u32[]{:S(2)}, u32[]{:S(2)}) collective-permute-start(bf16[512,2048]{1,0:T(8,128)(2,1)S(1)} %bitcast.17), channel_id=1, source_target_pairs={{0,1},{1,0},{2,3},{3,2},{4,5},{5,4},{6,7},{7,6},{8,9},{9,8},{10,11... | collective-permute-start | bytes 6291464 | tf_op jit(solution)/shard_map/ppermute | solution.py:147
  52.8 1.7 %collective-permute-done.2.refs_3_ = bf16[4,64,512]{2,1,0:T(8,128)(2,1)S(1)} collective-permute-done((bf16[4,64,512]{2,1,0:T(8,128)(2,1)S(1)}, bf16[4,64,512]{2,1,0:T(8,128)(2,1)S(1)}, u32[]{:S(2)}, u32[]{:S(2)}) %collective-permute-start.2) | collective-permute-done | bytes 262176 | tf_op jit(solution)/shard_map/ppermute | solution.py:141
  54.6 2.1 %collective-permute-done.4.refs_5_ = bf16[4,64,512]{2,1,0:T(8,128)(2,1)S(1)} collective-permute-done((bf16[4,64,512]{2,1,0:T(8,128)(2,1)S(1)}, bf16[4,64,512]{2,1,0:T(8,128)(2,1)S(1)}, u32[]{:S(2)}, u32[]{:S(2)}) %collective-permute-start.4) | collective-permute-done | bytes 262176 | tf_op jit(solution)/shard_map/ppermute | solution.py:143
  56.7 2.8 %collective-permute-done.5.refs_6_ = bf16[4,64,512]{2,1,0:T(8,128)(2,1)S(1)} collective-permute-done((bf16[4,64,512]{2,1,0:T(8,128)(2,1)S(1)}, bf16[4,64,512]{2,1,0:T(8,128)(2,1)S(1)}, u32[]{:S(2)}, u32[]{:S(2)}) %collective-permute-start.5) | collective-permute-done | bytes 262176 | tf_op jit(solution)/shard_map/ppermute | solution.py:144
  59.5 2.7 %collective-permute-done.6.refs_7_ = bf16[512,2048]{1,0:T(8,128)(2,1)S(1)} collective-permute-done((bf16[512,2048]{1,0:T(8,128)(2,1)}, bf16[512,2048]{1,0:T(8,128)(2,1)S(1)}, u32[]{:S(2)}, u32[]{:S(2)}) %collective-permute-start.6) | collective-permute-done | bytes 2097184 | tf_op jit(solution)/shard_map/ppermute | solution.py:136
  62.2 1.9 %collective-permute-start.7 = (bf16[512,2048]{1,0:T(8,128)(2,1)S(1)}, bf16[512,2048]{1,0:T(8,128)(2,1)S(1)}, u32[]{:S(2)}, u32[]{:S(2)}) collective-permute-start(bf16[512,2048]{1,0:T(8,128)(2,1)S(1)} %collective-permute-done.6.refs_7_), channel_id=1, source_target_pairs={{0,1},{1,0},{2,3},{3,2},{4,5},{5,4},{6,7},{7,6},{8,9},{9,8},{10,11... | collective-permute-start | bytes 6291464 | tf_op jit(solution)/shard_map/ppermute | solution.py:148
  64.1 0.0 collective-permute-done.8.refs_8_
  64.1 5.2 %shard_map.68.refs_9_ = bf16[4,128,2048]{2,1,0:T(8,128)(2,1)S(1)} custom-call(bf16[4,128,512]{2,1,0:T(8,128)(2,1)S(1)} %all_to_all.5.refs_0_, bf16[4,64,512]{2,1,0:T(8,128)(2,1)S(1)} %collective-permute-done.refs_1_, bf16[4,64,512]{2,1,0:T(8,128)(2,1)S(1)} %collective-permute-done.1.refs_2_, bf16[4,64,512]{2,1,0:T(8,128)(2,1)S(1)} %collective-permute-done.2.refs_3_, ...), custom_call_target="tpu_custom_call" | custom-call | flops 2147483648 | bytes 9437184 | tf_op jit(solution)/shard_map/pallas_call | solution.py:76
  69.3 0.0 collective-permute-done.7.refs_8_
  69.3 3.7 %shard_map.70 = (bf16[2,128,1024]{2,1,0:T(8,128)(2,1)S(1)}, bf16[2,128,1024]{2,1,0:T(8,128)(2,1)S(1)}) custom-call(bf16[4,128,512]{2,1,0:T(8,128)(2,1)S(1)} %all_to_all.5.refs_0_, bf16[4,64,512]{2,1,0:T(8,128)(2,1)S(1)} %collective-permute-done.refs_1_, bf16[4,64,512]{2,1,0:T(8,128)(2,1)S(1)} %collective-permute-done.1.refs_2_, ...), custom_call_target="tpu_custom_call" | custom-call | flops 1073741824 | bytes 7340032 | tf_op jit(solution)/shard_map/pallas_call | solution.py:76
  73.0 3.5 %collective-permute-start.9 = (bf16[2,128,1024]{2,1,0:T(8,128)(2,1)S(1)}, bf16[2,128,1024]{2,1,0:T(8,128)(2,1)S(1)}, u32[]{:S(2)}, u32[]{:S(2)}) collective-permute-start(bf16[2,128,1024]{2,1,0:T(8,128)(2,1)S(1)} %get-tuple-element.16), channel_id=1, source_target_pairs={{0,8},{1,9},{2,10},{3,11},{4,12},{5,13},{6,14},{7,15},{8,0},{9,1},... | collective-permute-start | bytes 1572872 | tf_op jit(solution)/shard_map/ppermute | solution.py:156
  76.5 4.7 %collective-permute-start.11 = (bf16[2,128,1024]{2,1,0:T(8,128)(2,1)S(1)}, bf16[2,128,1024]{2,1,0:T(8,128)(2,1)S(1)}, u32[]{:S(2)}, u32[]{:S(2)}) collective-permute-start(bf16[2,128,1024]{2,1,0:T(8,128)(2,1)S(1)} %get-tuple-element.20), channel_id=1, source_target_pairs={{0,6},{1,7},{2,4},{3,5},{4,2},{5,3},{6,0},{7,1},{8,14},{9,15},{10,... | collective-permute-start | bytes 1572872 | tf_op jit(solution)/shard_map/ppermute | solution.py:155
  81.2 3.7 %shard_map.69 = (bf16[2,128,1024]{2,1,0:T(8,128)(2,1)S(1)}, bf16[2,128,1024]{2,1,0:T(8,128)(2,1)S(1)}) custom-call(bf16[4,128,512]{2,1,0:T(8,128)(2,1)S(1)} %all_to_all.5.refs_0_, bf16[4,64,512]{2,1,0:T(8,128)(2,1)S(1)} %collective-permute-done.refs_1_, bf16[4,64,512]{2,1,0:T(8,128)(2,1)S(1)} %collective-permute-done.1.refs_2_, ...), custom_call_target="tpu_custom_call" | custom-call | flops 1073741824 | bytes 7340032 | tf_op jit(solution)/shard_map/pallas_call | solution.py:76
  84.9 4.3 %collective-permute-done.9.got = bf16[2,128,1024]{2,1,0:T(8,128)(2,1)S(1)} collective-permute-done((bf16[2,128,1024]{2,1,0:T(8,128)(2,1)S(1)}, bf16[2,128,1024]{2,1,0:T(8,128)(2,1)S(1)}, u32[]{:S(2)}, u32[]{:S(2)}) %collective-permute-start.9) | collective-permute-done | bytes 524320 | tf_op jit(solution)/shard_map/ppermute | solution.py:156
  89.2 0.1 shard_map.71
  89.4 0.0 copy-start.2
  89.4 4.8 %collective-permute-start.10 = (bf16[128,1024]{1,0:T(8,128)(2,1)S(1)}, bf16[128,1024]{1,0:T(8,128)(2,1)S(1)}, u32[]{:S(2)}, u32[]{:S(2)}) collective-permute-start(bf16[128,1024]{1,0:T(8,128)(2,1)S(1)} %get-tuple-element.18), channel_id=1, source_target_pairs={{0,6},{1,7},{2,4},{3,5},{4,2},{5,3},{6,0},{7,1},{8,14},{9,15},{10,... | collective-permute-start | bytes 786440 | tf_op jit(solution)/shard_map/ppermute | solution.py:159
  94.8 0.0 collective-permute-done.11.got
  94.8 0.1 shard_map.72
  95.0 3.5 %collective-permute-start.12 = (bf16[128,1024]{1,0:T(8,128)(2,1)S(1)}, bf16[128,1024]{1,0:T(8,128)(2,1)S(1)}, u32[]{:S(2)}, u32[]{:S(2)}) collective-permute-start(bf16[128,1024]{1,0:T(8,128)(2,1)S(1)} %get-tuple-element.22), channel_id=1, source_target_pairs={{0,8},{1,9},{2,10},{3,11},{4,12},{5,13},{6,14},{7,15},{8,0},{9,1},... | collective-permute-start | bytes 786440 | tf_op jit(solution)/shard_map/ppermute | solution.py:160
  98.5 2.0 %collective-permute-done.10 = bf16[128,1024]{1,0:T(8,128)(2,1)S(1)} collective-permute-done((bf16[128,1024]{1,0:T(8,128)(2,1)S(1)}, bf16[128,1024]{1,0:T(8,128)(2,1)S(1)}, u32[]{:S(2)}, u32[]{:S(2)}) %collective-permute-start.10) | collective-permute-done | bytes 262176 | tf_op jit(solution)/shard_map/ppermute | solution.py:159
  100.5 0.1 convert_add_fusion.1
  100.6 3.9 %collective-permute-done.12 = bf16[128,1024]{1,0:T(8,128)(2,1)S(1)} collective-permute-done((bf16[128,1024]{1,0:T(8,128)(2,1)S(1)}, bf16[128,1024]{1,0:T(8,128)(2,1)S(1)}, u32[]{:S(2)}, u32[]{:S(2)}) %collective-permute-start.12) | collective-permute-done | bytes 262176 | tf_op jit(solution)/shard_map/ppermute | solution.py:160
  104.5 0.1 convert_add_fusion
  104.6 0.0 copy-done.2
  104.6 0.3 fusion.2
  104.9 4.3 %collective-permute-start.13 = (bf16[128,2048]{1,0:T(8,128)(2,1)S(1)}, bf16[128,2048]{1,0:T(8,128)(2,1)S(1)}, u32[]{:S(2)}, u32[]{:S(2)}) collective-permute-start(bf16[128,2048]{1,0:T(8,128)(2,1)S(1)} %get-tuple-element.24), channel_id=1, source_target_pairs={{0,64},{64,128},{128,192},{192,256},{256,320},{320,384},{384,448},... | collective-permute-start | bytes 1572872 | tf_op jit(solution)/shard_map/ppermute | solution.py:175
  109.2 0.0 copy-done
  109.2 12.5 %psum.7 = f32[1,128]{1,0:T(1,128)S(1)} all-reduce(f32[1,128]{1,0:T(1,128)S(1)} %bitcast.22), channel_id=1, replica_groups=mesh['section'=12,'dp'=4,'tensor'=16] {'dp'}, use_global_device_ids=true, to_apply=%region_1.2 | all-reduce | flops 128 | bytes 1024 | tf_op jit(solution)/shard_map/psum | solution.py:176
  121.7 1.8 %collective-permute-done.13 = bf16[128,2048]{1,0:T(8,128)(2,1)S(1)} collective-permute-done((bf16[128,2048]{1,0:T(8,128)(2,1)S(1)}, bf16[128,2048]{1,0:T(8,128)(2,1)S(1)}, u32[]{:S(2)}, u32[]{:S(2)}) %collective-permute-start.13) | collective-permute-done | bytes 524320 | tf_op jit(solution)/shard_map/ppermute | solution.py:175
  123.5 0.9 fusion.1
  124.5 0.8 copy.9
  (4 shorter events, 0.1 us)
Async XLA Ops:
  0.6 108.5 %copy-start = (f32[1,8192]{1,0:T(1,128)S(1)}, f32[1,8192]{1,0:T(1,128)}, u32[]{:S(2)}) copy-start(f32[1,8192]{1,0:T(1,128)} %param.8) | copy-start | bytes 98308
  0.6 50.3 %copy-start.1 = (bf16[1,512,2048]{2,1,0:T(8,128)(2,1)S(1)}, bf16[1,512,2048]{2,1,0:T(8,128)(2,1)}, u32[]{:S(2)}) copy-start(bf16[1,512,2048]{2,1,0:T(8,128)(2,1)} %param.7) | copy-start | bytes 6291460
  13.1 49.1 %collective-permute-start.6 = (bf16[512,2048]{1,0:T(8,128)(2,1)}, bf16[512,2048]{1,0:T(8,128)(2,1)S(1)}, u32[]{:S(2)}, u32[]{:S(2)}) collective-permute-start(bf16[512,2048]{1,0:T(8,128)(2,1)} %bitcast.16), channel_id=1, source_target_pairs={{0,2},{1,3},{2,0},{3,1},{4,6},{5,7},{6,4},{7,5},{8,10},{9,11},{10,... | collective-permute-start | bytes 6291464 | tf_op jit(solution)/shard_map/ppermute | solution.py:136
  15.4 20.8 %collective-permute-start = (bf16[4,64,512]{2,1,0:T(8,128)(2,1)S(1)}, bf16[4,64,512]{2,1,0:T(8,128)(2,1)S(1)}, u32[]{:S(2)}, u32[]{:S(2)}) collective-permute-start(bf16[4,64,512]{2,1,0:T(8,128)(2,1)S(1)} %get-tuple-element.28), channel_id=1, source_target_pairs={{0,16},{16,32},{32,48},{48,0},{1,17},{17,33},{33,49},{49,1},{2,18}... | collective-permute-start | bytes 786440 | tf_op jit(solution)/shard_map/ppermute | solution.py:139
  21.0 25.1 %collective-permute-start.3 = (bf16[4,64,512]{2,1,0:T(8,128)(2,1)S(1)}, bf16[4,64,512]{2,1,0:T(8,128)(2,1)S(1)}, u32[]{:S(2)}, u32[]{:S(2)}) collective-permute-start(bf16[4,64,512]{2,1,0:T(8,128)(2,1)S(1)} %get-tuple-element.27), channel_id=1, source_target_pairs={{0,48},{16,0},{32,16},{48,32},{1,49},{17,1},{33,17},{49,33},{2,50}... | collective-permute-start | bytes 786440 | tf_op jit(solution)/shard_map/ppermute | solution.py:140
  24.6 26.3 %collective-permute-start.1 = (bf16[4,64,512]{2,1,0:T(8,128)(2,1)S(1)}, bf16[4,64,512]{2,1,0:T(8,128)(2,1)S(1)}, u32[]{:S(2)}, u32[]{:S(2)}) collective-permute-start(bf16[4,64,512]{2,1,0:T(8,128)(2,1)S(1)} %get-tuple-element.27), channel_id=1, source_target_pairs={{0,16},{16,32},{32,48},{48,0},{1,17},{17,33},{33,49},{49,1},{2,18}... | collective-permute-start | bytes 786440 | tf_op jit(solution)/shard_map/ppermute | solution.py:142
  27.8 26.8 %collective-permute-start.2 = (bf16[4,64,512]{2,1,0:T(8,128)(2,1)S(1)}, bf16[4,64,512]{2,1,0:T(8,128)(2,1)S(1)}, u32[]{:S(2)}, u32[]{:S(2)}) collective-permute-start(bf16[4,64,512]{2,1,0:T(8,128)(2,1)S(1)} %get-tuple-element.28), channel_id=1, source_target_pairs={{0,48},{16,0},{32,16},{48,32},{1,49},{17,1},{33,17},{49,33},{2,50}... | collective-permute-start | bytes 786440 | tf_op jit(solution)/shard_map/ppermute | solution.py:141
  36.2 20.5 %collective-permute-start.4 = (bf16[4,64,512]{2,1,0:T(8,128)(2,1)S(1)}, bf16[4,64,512]{2,1,0:T(8,128)(2,1)S(1)}, u32[]{:S(2)}, u32[]{:S(2)}) collective-permute-start(bf16[4,64,512]{2,1,0:T(8,128)(2,1)S(1)} %collective-permute-done.refs_1_), channel_id=1, source_target_pairs={{0,16},{16,32},{32,48},{48,0},{1,17},{17,33},{33,49},{49,1},{2,18}... | collective-permute-start | bytes 786440 | tf_op jit(solution)/shard_map/ppermute | solution.py:143
  46.1 13.4 %collective-permute-start.5 = (bf16[4,64,512]{2,1,0:T(8,128)(2,1)S(1)}, bf16[4,64,512]{2,1,0:T(8,128)(2,1)S(1)}, u32[]{:S(2)}, u32[]{:S(2)}) collective-permute-start(bf16[4,64,512]{2,1,0:T(8,128)(2,1)S(1)} %collective-permute-done.3.refs_4_), channel_id=1, source_target_pairs={{0,48},{16,0},{32,16},{48,32},{1,49},{17,1},{33,17},{49,33},{2,50}... | collective-permute-start | bytes 786440 | tf_op jit(solution)/shard_map/ppermute | solution.py:144
  50.9 13.2 %collective-permute-start.8 = (bf16[512,2048]{1,0:T(8,128)(2,1)S(1)}, bf16[512,2048]{1,0:T(8,128)(2,1)S(1)}, u32[]{:S(2)}, u32[]{:S(2)}) collective-permute-start(bf16[512,2048]{1,0:T(8,128)(2,1)S(1)} %bitcast.17), channel_id=1, source_target_pairs={{0,1},{1,0},{2,3},{3,2},{4,5},{5,4},{6,7},{7,6},{8,9},{9,8},{10,11... | collective-permute-start | bytes 6291464 | tf_op jit(solution)/shard_map/ppermute | solution.py:147
  62.2 7.1 %collective-permute-start.7 = (bf16[512,2048]{1,0:T(8,128)(2,1)S(1)}, bf16[512,2048]{1,0:T(8,128)(2,1)S(1)}, u32[]{:S(2)}, u32[]{:S(2)}) collective-permute-start(bf16[512,2048]{1,0:T(8,128)(2,1)S(1)} %collective-permute-done.6.refs_7_), channel_id=1, source_target_pairs={{0,1},{1,0},{2,3},{3,2},{4,5},{5,4},{6,7},{7,6},{8,9},{9,8},{10,11... | collective-permute-start | bytes 6291464 | tf_op jit(solution)/shard_map/ppermute | solution.py:148
  73.0 16.2 %collective-permute-start.9 = (bf16[2,128,1024]{2,1,0:T(8,128)(2,1)S(1)}, bf16[2,128,1024]{2,1,0:T(8,128)(2,1)S(1)}, u32[]{:S(2)}, u32[]{:S(2)}) collective-permute-start(bf16[2,128,1024]{2,1,0:T(8,128)(2,1)S(1)} %get-tuple-element.16), channel_id=1, source_target_pairs={{0,8},{1,9},{2,10},{3,11},{4,12},{5,13},{6,14},{7,15},{8,0},{9,1},... | collective-permute-start | bytes 1572872 | tf_op jit(solution)/shard_map/ppermute | solution.py:156
  76.5 18.3 %collective-permute-start.11 = (bf16[2,128,1024]{2,1,0:T(8,128)(2,1)S(1)}, bf16[2,128,1024]{2,1,0:T(8,128)(2,1)S(1)}, u32[]{:S(2)}, u32[]{:S(2)}) collective-permute-start(bf16[2,128,1024]{2,1,0:T(8,128)(2,1)S(1)} %get-tuple-element.20), channel_id=1, source_target_pairs={{0,6},{1,7},{2,4},{3,5},{4,2},{5,3},{6,0},{7,1},{8,14},{9,15},{10,... | collective-permute-start | bytes 1572872 | tf_op jit(solution)/shard_map/ppermute | solution.py:155
  89.4 15.2 %copy-start.2 = (bf16[1,128,2048]{2,1,0:T(8,128)(2,1)S(1)}, bf16[1,128,2048]{2,1,0:T(8,128)(2,1)}, u32[]{:S(2)}) copy-start(bf16[1,128,2048]{2,1,0:T(8,128)(2,1)} %param.6) | copy-start | bytes 1572868
  89.4 11.2 %collective-permute-start.10 = (bf16[128,1024]{1,0:T(8,128)(2,1)S(1)}, bf16[128,1024]{1,0:T(8,128)(2,1)S(1)}, u32[]{:S(2)}, u32[]{:S(2)}) collective-permute-start(bf16[128,1024]{1,0:T(8,128)(2,1)S(1)} %get-tuple-element.18), channel_id=1, source_target_pairs={{0,6},{1,7},{2,4},{3,5},{4,2},{5,3},{6,0},{7,1},{8,14},{9,15},{10,... | collective-permute-start | bytes 786440 | tf_op jit(solution)/shard_map/ppermute | solution.py:159
  95.0 9.5 %collective-permute-start.12 = (bf16[128,1024]{1,0:T(8,128)(2,1)S(1)}, bf16[128,1024]{1,0:T(8,128)(2,1)S(1)}, u32[]{:S(2)}, u32[]{:S(2)}) collective-permute-start(bf16[128,1024]{1,0:T(8,128)(2,1)S(1)} %get-tuple-element.22), channel_id=1, source_target_pairs={{0,8},{1,9},{2,10},{3,11},{4,12},{5,13},{6,14},{7,15},{8,0},{9,1},... | collective-permute-start | bytes 786440 | tf_op jit(solution)/shard_map/ppermute | solution.py:160
  104.9 18.6 %collective-permute-start.13 = (bf16[128,2048]{1,0:T(8,128)(2,1)S(1)}, bf16[128,2048]{1,0:T(8,128)(2,1)S(1)}, u32[]{:S(2)}, u32[]{:S(2)}) collective-permute-start(bf16[128,2048]{1,0:T(8,128)(2,1)S(1)} %get-tuple-element.24), channel_id=1, source_target_pairs={{0,64},{64,128},{128,192},{192,256},{256,320},{320,384},{384,448},... | collective-permute-start | bytes 1572872 | tf_op jit(solution)/shard_map/ppermute | solution.py:175

commit v4 on v3

--- a/solution.py
+++ b/solution.py
@@ -9,7 +9,13 @@
 
 WIDE = 512
 CUT = 1024
+TILES = (512, 512, 512, 512)
 PARTS = 4
+
+
+def tiles_of(columns, added):
+    widths = TILES if added else (WIDE,) * (columns // WIDE)
+    return [(sum(widths[:i]), width) for i, width in enumerate(widths)]
 
 
 def project(*refs, places, first_rel, going):
@@ -29,37 +35,38 @@
 
     for source, (shift, begin) in zip(sources, places):
         slot = lax.rem(d + shift, PARTS)
-        order = me ^ (((slot % 2) ^ xh) * 2)
         for i in range(2):
-            fetch(source.at[order ^ (first_rel + i)], rows.at[slot, pl.ds(begin, source.shape[1]), pl.ds(i * k, k)])
+            fetch(source.at[first_rel + i], rows.at[slot, pl.ds(begin, source.shape[1]), pl.ds(i * k, k)])
     first = len(copies)
     if going:
         wanted = ([(1 - ylo) * 2 + i for i in range(2)], [i * 2 + 1 - xh for i in range(2)])
     else:
         wanted = ([ylo * 2 + i for i in range(2)], [i * 2 + xh for i in range(2)])
     each = 4 if added else 2
-    for at in range(0, columns, WIDE):
+    tiles = tiles_of(columns, added)
+    for at, width in tiles:
         for i, weight in enumerate(weights):
-            fetch(weight.at[:, pl.ds(at, WIDE)], held.at[pl.ds(i * k, k), pl.ds(at, WIDE)])
+            fetch(weight.at[:, pl.ds(at, width)], held.at[pl.ds(i * k, k), pl.ds(at, width)])
         if added:
-            for i, block in enumerate(wanted[at // CUT]):
-                fetch(before.at[block, :, pl.ds(at, WIDE)], base.at[i, :, pl.ds(at, WIDE)])
+            for i, block in enumerate(wanted[at >= CUT]):
+                fetch(before.at[block, :, pl.ds(at, width)], base.at[i, :, pl.ds(at, width)])
     for copy in copies[:first]:
         copy.wait()
     sent = []
-    for j, at in enumerate(range(0, columns, WIDE)):
+    for j, (at, width) in enumerate(tiles):
+        here = pl.ds(at, width)
         if not added:
             lhs = rows[...].reshape(-1, 2 * k)
-        elif at % CUT == 0:
-            lhs = jnp.concatenate([rows[block] for block in wanted[at // CUT]], axis=0)
+        elif at in (0, CUT):
+            lhs = jnp.concatenate([rows[block] for block in wanted[at >= CUT]], axis=0)
         for copy in copies[first + each * j:first + each * (j + 1)]:
             copy.wait()
-        value = jnp.dot(lhs, held[:, at:at + WIDE], preferred_element_type=jnp.float32).reshape(result.shape[0], -1, WIDE)
+        value = jnp.dot(lhs, held[:, here], preferred_element_type=jnp.float32).reshape(result.shape[0], -1, width)
         if added:
-            value += base[:, :, at:at + WIDE].astype(jnp.float32)
-        result[:, :, at:at + WIDE] = value.astype(result.dtype)
-        target, to = (outs[at // CUT], at % CUT) if added else (outs[0], at)
-        sent.append(pltpu.make_async_copy(result.at[:, :, pl.ds(at, WIDE)], target.at[:, :, pl.ds(to, WIDE)], out_sem.at[j]))
+            value += base[:, :, here].astype(jnp.float32)
+        result[:, :, here] = value.astype(result.dtype)
+        target, to = (outs[1], at - CUT) if added and at >= CUT else (outs[0], at)
+        sent.append(pltpu.make_async_copy(result.at[:, :, here], target.at[:, :, pl.ds(to, width)], out_sem.at[j]))
         sent[-1].start()
     for copy in sent:
         copy.wait()
@@ -67,10 +74,10 @@
 
 def projected(places, first_rel, sources, weights, before, rows, going=None):
     k, columns = weights[0].shape
-    tiles = columns // WIDE
     added = going is not None
+    tiles = len(tiles_of(columns, added))
     parts = 2 if added else PARTS
-    shapes = [(2, rows, CUT)] * 2 if added else [(PARTS, rows, columns)]
+    shapes = [(2, rows, CUT), (2, rows, columns - CUT)] if added else [(PARTS, rows, columns)]
     anywhere = pl.BlockSpec(memory_space=pl.ANY)
     operands = [*sources, *weights] + ([before] if added else [])
     return pl.pallas_call(
@@ -131,9 +138,15 @@
     quads = [[16 * dd + 4 * g + (i ^ (2 * ((dd ^ g) % 2))) for i in range(4)] for dd in range(4) for g in range(4)]
     across = [[4 * g + i for g in range(4)] for i in range(4)]
 
-    tokens = lax.all_to_all(context.reshape(4, rows, width), ("dp", "tensor"), 0, 0, axis_index_groups=quads, tiled=True)
+    pieces = context.reshape(4, rows, width)
+    flip = 2 * ((d % 2) ^ ((t // 4) % 2))
+    mine, along, across, corner = (lax.dynamic_index_in_dim(pieces, (t % 4) ^ rel ^ flip, 0, keepdims=False) for rel in range(4))
+    got = lax.ppermute(jnp.stack([across, corner]), "tensor", pair)
+    across, passed = got[0], got[1]
+    along, corner = lax.ppermute(jnp.stack([along, passed]), "tensor", swap)
+    tokens = jnp.stack([mine, along, across, corner])
     weight = out_weight[0]
-    near = [lax.ppermute(after(weight, tokens), "tensor", pair)]
+    near = [lax.ppermute(after(weight, got), "tensor", pair)]
 
     own_a, own_b = tokens[:, :r], tokens[:, r:]
     right_a = lax.ppermute(own_a, "dp", up)

time: 126 us -> 125 us (level)
  the two profiles are of different devices: /device:TPU:64 before, /device:TPU:512 now
where the time goes in v4:
time: 125 us
  starting transfers between devices  59.1 us (47%)
  waiting for transfers between devices  37.7 us (30%)
  Pallas kernels  12.7 us (10%)
  blocking collectives  9.91 us (8%)
  local copies, waits for them, and re-layouts  2.03 us (2%)
  between operations  1.67 us (1%)
  other arithmetic  1.48 us (1%)
    pallas_call x3, Pallas kernels, projected(): pl.pallas_call(functools.partial(project, places=places, first_rel=first_...  12.5 us
    psum x1, blocking collectives, on_device(): square = lax.psum(square, 'dp')  9.91 us
    ppermute x1, starting transfers between devices, on_device(): got_a = lax.ppermute(send_a, 'tensor', over_y)  8.11 us
    ppermute x1, waiting for transfers between devices, on_device(): left_b = lax.ppermute(own_b, 'dp', down)  7.03 us
    ppermute x1, waiting for transfers between devices, on_device(): got = lax.ppermute(jnp.stack([across, corner]), 'tensor', pair)  6.53 us
    ppermute x1, waiting for transfers between devices, on_device(): got_a = lax.ppermute(send_a, 'tensor', over_y)  4.88 us
    ppermute x1, waiting for transfers between devices, on_device(): far_b = lax.ppermute(left_b, 'dp', down)  4.5 us
    ppermute x1, starting transfers between devices, on_device(): right_a = lax.ppermute(own_a, 'dp', up)  4.5 us
  transfers between devices with their start and end apart: 16, of which 12 were waited for; matrix products, arithmetic and copies ran while one was open for 0% of the time, Pallas kernels for 7%

profile of v4, /device:TPU:512, one launch (start us, length us, event | category | flops | bytes accessed | tf_op | source)
XLA Modules:
  0.0 124.6 jit_solution(1468627129315170851)
XLA Ops:
  0.6 0.0 copy-start
  0.7 1.1 constant_dynamic-slice_fusion.4
  1.9 0.0 copy-start.1
  1.9 3.5 %collective-permute-start = (bf16[2,128,512]{2,1,0:T(8,128)(2,1)S(1)}, bf16[2,128,512]{2,1,0:T(8,128)(2,1)S(1)}, u32[]{:S(2)}, u32[]{:S(2)}) collective-permute-start(bf16[2,128,512]{2,1,0:T(8,128)(2,1)S(1)} %pad_maximum_fusion.1), channel_id=1, source_target_pairs={{0,2},{1,3},{2,0},{3,1},{4,6},{5,7},{6,4},{7,5},{8,10},{9,11},{10,... | collective-permute-start | bytes 786440 | tf_op jit(solution)/shard_map/ppermute | solution.py:144
  5.4 6.5 %collective-permute-done = bf16[2,128,512]{2,1,0:T(8,128)(2,1)S(1)} collective-permute-done((bf16[2,128,512]{2,1,0:T(8,128)(2,1)S(1)}, bf16[2,128,512]{2,1,0:T(8,128)(2,1)S(1)}, u32[]{:S(2)}, u32[]{:S(2)}) %collective-permute-start) | collective-permute-done | bytes 262176 | tf_op jit(solution)/shard_map/ppermute | solution.py:144
  12.0 3.4 %collective-permute-start.8 = (bf16[512,2048]{1,0:T(8,128)(2,1)}, bf16[512,2048]{1,0:T(8,128)(2,1)S(1)}, u32[]{:S(2)}, u32[]{:S(2)}) collective-permute-start(bf16[512,2048]{1,0:T(8,128)(2,1)} %bitcast.16), channel_id=1, source_target_pairs={{0,2},{1,3},{2,0},{3,1},{4,6},{5,7},{6,4},{7,5},{8,10},{9,11},{10,... | collective-permute-start | bytes 6291464 | tf_op jit(solution)/shard_map/ppermute | solution.py:149
  15.4 1.9 %collective-permute-start.1 = (bf16[2,128,512]{2,1,0:T(8,128)(2,1)S(1)}, bf16[2,128,512]{2,1,0:T(8,128)(2,1)S(1)}, u32[]{:S(2)}, u32[]{:S(2)}) collective-permute-start(bf16[2,128,512]{2,1,0:T(8,128)(2,1)S(1)} %pad_maximum_fusion.2), channel_id=1, source_target_pairs={{0,1},{1,0},{2,3},{3,2},{4,5},{5,4},{6,7},{7,6},{8,9},{9,8},{10,11... | collective-permute-start | bytes 786440 | tf_op jit(solution)/shard_map/ppermute | solution.py:146
  17.4 1.5 %collective-permute-done.1 = bf16[2,128,512]{2,1,0:T(8,128)(2,1)S(1)} collective-permute-done((bf16[2,128,512]{2,1,0:T(8,128)(2,1)S(1)}, bf16[2,128,512]{2,1,0:T(8,128)(2,1)S(1)}, u32[]{:S(2)}, u32[]{:S(2)}) %collective-permute-start.1) | collective-permute-done | bytes 262176 | tf_op jit(solution)/shard_map/ppermute | solution.py:146
  18.9 0.1 pad_maximum_fusion.refs_0_
  19.0 4.5 %collective-permute-start.2 = (bf16[4,64,512]{2,1,0:T(8,128)(2,1)S(1)}, bf16[4,64,512]{2,1,0:T(8,128)(2,1)S(1)}, u32[]{:S(2)}, u32[]{:S(2)}) collective-permute-start(bf16[4,64,512]{2,1,0:T(8,128)(2,1)S(1)} %get-tuple-element.28), channel_id=1, source_target_pairs={{0,16},{16,32},{32,48},{48,0},{1,17},{17,33},{33,49},{49,1},{2,18}... | collective-permute-start | bytes 786440 | tf_op jit(solution)/shard_map/ppermute | solution.py:152
  23.5 3.6 %collective-permute-start.5 = (bf16[4,64,512]{2,1,0:T(8,128)(2,1)S(1)}, bf16[4,64,512]{2,1,0:T(8,128)(2,1)S(1)}, u32[]{:S(2)}, u32[]{:S(2)}) collective-permute-start(bf16[4,64,512]{2,1,0:T(8,128)(2,1)S(1)} %get-tuple-element.27), channel_id=1, source_target_pairs={{0,48},{16,0},{32,16},{48,32},{1,49},{17,1},{33,17},{49,33},{2,50}... | collective-permute-start | bytes 786440 | tf_op jit(solution)/shard_map/ppermute | solution.py:153
  27.1 4.0 %collective-permute-start.3 = (bf16[4,64,512]{2,1,0:T(8,128)(2,1)S(1)}, bf16[4,64,512]{2,1,0:T(8,128)(2,1)S(1)}, u32[]{:S(2)}, u32[]{:S(2)}) collective-permute-start(bf16[4,64,512]{2,1,0:T(8,128)(2,1)S(1)} %get-tuple-element.27), channel_id=1, source_target_pairs={{0,16},{16,32},{32,48},{48,0},{1,17},{17,33},{33,49},{49,1},{2,18}... | collective-permute-start | bytes 786440 | tf_op jit(solution)/shard_map/ppermute | solution.py:155
  31.2 3.9 %collective-permute-start.4 = (bf16[4,64,512]{2,1,0:T(8,128)(2,1)S(1)}, bf16[4,64,512]{2,1,0:T(8,128)(2,1)S(1)}, u32[]{:S(2)}, u32[]{:S(2)}) collective-permute-start(bf16[4,64,512]{2,1,0:T(8,128)(2,1)S(1)} %get-tuple-element.28), channel_id=1, source_target_pairs={{0,48},{16,0},{32,16},{48,32},{1,49},{17,1},{33,17},{49,33},{2,50}... | collective-permute-start | bytes 786440 | tf_op jit(solution)/shard_map/ppermute | solution.py:154
  35.1 0.1 collective-permute-done.2.refs_1_
  35.2 3.9 %collective-permute-start.6 = (bf16[4,64,512]{2,1,0:T(8,128)(2,1)S(1)}, bf16[4,64,512]{2,1,0:T(8,128)(2,1)S(1)}, u32[]{:S(2)}, u32[]{:S(2)}) collective-permute-start(bf16[4,64,512]{2,1,0:T(8,128)(2,1)S(1)} %collective-permute-done.2.refs_1_), channel_id=1, source_target_pairs={{0,16},{16,32},{32,48},{48,0},{1,17},{17,33},{33,49},{49,1},{2,18}... | collective-permute-start | bytes 786440 | tf_op jit(solution)/shard_map/ppermute | solution.py:156
  39.1 7.0 %collective-permute-done.5.refs_4_ = bf16[4,64,512]{2,1,0:T(8,128)(2,1)S(1)} collective-permute-done((bf16[4,64,512]{2,1,0:T(8,128)(2,1)S(1)}, bf16[4,64,512]{2,1,0:T(8,128)(2,1)S(1)}, u32[]{:S(2)}, u32[]{:S(2)}) %collective-permute-start.5) | collective-permute-done | bytes 262176 | tf_op jit(solution)/shard_map/ppermute | solution.py:153
  46.2 3.2 %collective-permute-start.7 = (bf16[4,64,512]{2,1,0:T(8,128)(2,1)S(1)}, bf16[4,64,512]{2,1,0:T(8,128)(2,1)S(1)}, u32[]{:S(2)}, u32[]{:S(2)}) collective-permute-start(bf16[4,64,512]{2,1,0:T(8,128)(2,1)S(1)} %collective-permute-done.5.refs_4_), channel_id=1, source_target_pairs={{0,48},{16,0},{32,16},{48,32},{1,49},{17,1},{33,17},{49,33},{2,50}... | collective-permute-start | bytes 786440 | tf_op jit(solution)/shard_map/ppermute | solution.py:157
  49.4 0.0 collective-permute-done.3.refs_2_
  49.4 1.9 %collective-permute-start.10 = (bf16[512,2048]{1,0:T(8,128)(2,1)S(1)}, bf16[512,2048]{1,0:T(8,128)(2,1)S(1)}, u32[]{:S(2)}, u32[]{:S(2)}) collective-permute-start(bf16[512,2048]{1,0:T(8,128)(2,1)S(1)} %bitcast.17), channel_id=1, source_target_pairs={{0,1},{1,0},{2,3},{3,2},{4,5},{5,4},{6,7},{7,6},{8,9},{9,8},{10,11... | collective-permute-start | bytes 6291464 | tf_op jit(solution)/shard_map/ppermute | solution.py:160
  51.3 2.1 %collective-permute-done.4.refs_3_ = bf16[4,64,512]{2,1,0:T(8,128)(2,1)S(1)} collective-permute-done((bf16[4,64,512]{2,1,0:T(8,128)(2,1)S(1)}, bf16[4,64,512]{2,1,0:T(8,128)(2,1)S(1)}, u32[]{:S(2)}, u32[]{:S(2)}) %collective-permute-start.4) | collective-permute-done | bytes 262176 | tf_op jit(solution)/shard_map/ppermute | solution.py:154
  53.4 1.6 %collective-permute-done.6.refs_5_ = bf16[4,64,512]{2,1,0:T(8,128)(2,1)S(1)} collective-permute-done((bf16[4,64,512]{2,1,0:T(8,128)(2,1)S(1)}, bf16[4,64,512]{2,1,0:T(8,128)(2,1)S(1)}, u32[]{:S(2)}, u32[]{:S(2)}) %collective-permute-start.6) | collective-permute-done | bytes 262176 | tf_op jit(solution)/shard_map/ppermute | solution.py:156
  55.0 4.5 %collective-permute-done.7.refs_6_ = bf16[4,64,512]{2,1,0:T(8,128)(2,1)S(1)} collective-permute-done((bf16[4,64,512]{2,1,0:T(8,128)(2,1)S(1)}, bf16[4,64,512]{2,1,0:T(8,128)(2,1)S(1)}, u32[]{:S(2)}, u32[]{:S(2)}) %collective-permute-start.7) | collective-permute-done | bytes 262176 | tf_op jit(solution)/shard_map/ppermute | solution.py:157
  59.5 1.1 collective-permute-done.8.refs_7_
  60.6 1.9 %collective-permute-start.9 = (bf16[512,2048]{1,0:T(8,128)(2,1)S(1)}, bf16[512,2048]{1,0:T(8,128)(2,1)S(1)}, u32[]{:S(2)}, u32[]{:S(2)}) collective-permute-start(bf16[512,2048]{1,0:T(8,128)(2,1)S(1)} %collective-permute-done.8.refs_7_), channel_id=1, source_target_pairs={{0,1},{1,0},{2,3},{3,2},{4,5},{5,4},{6,7},{7,6},{8,9},{9,8},{10,11... | collective-permute-start | bytes 6291464 | tf_op jit(solution)/shard_map/ppermute | solution.py:161
  62.5 0.0 collective-permute-done.10.refs_8_
  62.5 5.2 %shard_map.68.refs_9_ = bf16[4,128,2048]{2,1,0:T(8,128)(2,1)S(1)} custom-call(bf16[4,128,512]{2,1,0:T(8,128)(2,1)S(1)} %pad_maximum_fusion.refs_0_, bf16[4,64,512]{2,1,0:T(8,128)(2,1)S(1)} %collective-permute-done.2.refs_1_, bf16[4,64,512]{2,1,0:T(8,128)(2,1)S(1)} %collective-permute-done.3.refs_2_, bf16[4,64,512]{2,1,0:T(8,128)(2,1)S(1)} %collective-permute-done.4.refs_3_, ...), custom_call_target="tpu_custom_call" | custom-call | flops 2147483648 | bytes 9437184 | tf_op jit(solution)/shard_map/pallas_call | solution.py:83
  67.7 0.0 collective-permute-done.9.refs_8_
  67.7 3.7 %shard_map.70 = (bf16[2,128,1024]{2,1,0:T(8,128)(2,1)S(1)}, bf16[2,128,1024]{2,1,0:T(8,128)(2,1)S(1)}) custom-call(bf16[4,128,512]{2,1,0:T(8,128)(2,1)S(1)} %pad_maximum_fusion.refs_0_, bf16[4,64,512]{2,1,0:T(8,128)(2,1)S(1)} %collective-permute-done.2.refs_1_, bf16[4,64,512]{2,1,0:T(8,128)(2,1)S(1)} %collective-permute-done.3.refs_2_, ...), custom_call_target="tpu_custom_call" | custom-call | flops 1073741824 | bytes 7340032 | tf_op jit(solution)/shard_map/pallas_call | solution.py:83
  71.3 8.1 %collective-permute-start.11 = (bf16[2,128,1024]{2,1,0:T(8,128)(2,1)S(1)}, bf16[2,128,1024]{2,1,0:T(8,128)(2,1)S(1)}, u32[]{:S(2)}, u32[]{:S(2)}) collective-permute-start(bf16[2,128,1024]{2,1,0:T(8,128)(2,1)S(1)} %get-tuple-element.16), channel_id=1, source_target_pairs={{0,8},{1,9},{2,10},{3,11},{4,12},{5,13},{6,14},{7,15},{8,0},{9,1},... | collective-permute-start | bytes 1572872 | tf_op jit(solution)/shard_map/ppermute | solution.py:169
  79.5 4.0 %collective-permute-start.13 = (bf16[2,128,1024]{2,1,0:T(8,128)(2,1)S(1)}, bf16[2,128,1024]{2,1,0:T(8,128)(2,1)S(1)}, u32[]{:S(2)}, u32[]{:S(2)}) collective-permute-start(bf16[2,128,1024]{2,1,0:T(8,128)(2,1)S(1)} %get-tuple-element.20), channel_id=1, source_target_pairs={{0,6},{1,7},{2,4},{3,5},{4,2},{5,3},{6,0},{7,1},{8,14},{9,15},{10,... | collective-permute-start | bytes 1572872 | tf_op jit(solution)/shard_map/ppermute | solution.py:168
  83.5 3.7 %shard_map.69 = (bf16[2,128,1024]{2,1,0:T(8,128)(2,1)S(1)}, bf16[2,128,1024]{2,1,0:T(8,128)(2,1)S(1)}) custom-call(bf16[4,128,512]{2,1,0:T(8,128)(2,1)S(1)} %pad_maximum_fusion.refs_0_, bf16[4,64,512]{2,1,0:T(8,128)(2,1)S(1)} %collective-permute-done.2.refs_1_, bf16[4,64,512]{2,1,0:T(8,128)(2,1)S(1)} %collective-permute-done.3.refs_2_, ...), custom_call_target="tpu_custom_call" | custom-call | flops 1073741824 | bytes 7340032 | tf_op jit(solution)/shard_map/pallas_call | solution.py:83
  87.1 4.9 %collective-permute-done.11.got = bf16[2,128,1024]{2,1,0:T(8,128)(2,1)S(1)} collective-permute-done((bf16[2,128,1024]{2,1,0:T(8,128)(2,1)S(1)}, bf16[2,128,1024]{2,1,0:T(8,128)(2,1)S(1)}, u32[]{:S(2)}, u32[]{:S(2)}) %collective-permute-start.11) | collective-permute-done | bytes 524320 | tf_op jit(solution)/shard_map/ppermute | solution.py:169
  92.0 0.1 shard_map.71
  92.1 0.0 copy-start.2
  92.2 4.1 %collective-permute-start.12 = (bf16[128,1024]{1,0:T(8,128)(2,1)S(1)}, bf16[128,1024]{1,0:T(8,128)(2,1)S(1)}, u32[]{:S(2)}, u32[]{:S(2)}) collective-permute-start(bf16[128,1024]{1,0:T(8,128)(2,1)S(1)} %get-tuple-element.18), channel_id=1, source_target_pairs={{0,6},{1,7},{2,4},{3,5},{4,2},{5,3},{6,0},{7,1},{8,14},{9,15},{10,... | collective-permute-start | bytes 786440 | tf_op jit(solution)/shard_map/ppermute | solution.py:172
  97.0 0.0 collective-permute-done.13.got
  97.0 0.1 shard_map.72
  97.1 3.6 %collective-permute-start.14 = (bf16[128,1024]{1,0:T(8,128)(2,1)S(1)}, bf16[128,1024]{1,0:T(8,128)(2,1)S(1)}, u32[]{:S(2)}, u32[]{:S(2)}) collective-permute-start(bf16[128,1024]{1,0:T(8,128)(2,1)S(1)} %get-tuple-element.22), channel_id=1, source_target_pairs={{0,8},{1,9},{2,10},{3,11},{4,12},{5,13},{6,14},{7,15},{8,0},{9,1},... | collective-permute-start | bytes 786440 | tf_op jit(solution)/shard_map/ppermute | solution.py:173
  100.8 2.8 %collective-permute-done.12 = bf16[128,1024]{1,0:T(8,128)(2,1)S(1)} collective-permute-done((bf16[128,1024]{1,0:T(8,128)(2,1)S(1)}, bf16[128,1024]{1,0:T(8,128)(2,1)S(1)}, u32[]{:S(2)}, u32[]{:S(2)}) %collective-permute-start.12) | collective-permute-done | bytes 262176 | tf_op jit(solution)/shard_map/ppermute | solution.py:172
  103.5 0.1 convert_add_fusion.1
  103.6 3.3 %collective-permute-done.14 = bf16[128,1024]{1,0:T(8,128)(2,1)S(1)} collective-permute-done((bf16[128,1024]{1,0:T(8,128)(2,1)S(1)}, bf16[128,1024]{1,0:T(8,128)(2,1)S(1)}, u32[]{:S(2)}, u32[]{:S(2)}) %collective-permute-start.14) | collective-permute-done | bytes 262176 | tf_op jit(solution)/shard_map/ppermute | solution.py:173
  106.8 0.1 convert_add_fusion
  106.9 0.3 fusion.2
  107.2 3.4 %collective-permute-start.15 = (bf16[128,2048]{1,0:T(8,128)(2,1)S(1)}, bf16[128,2048]{1,0:T(8,128)(2,1)S(1)}, u32[]{:S(2)}, u32[]{:S(2)}) collective-permute-start(bf16[128,2048]{1,0:T(8,128)(2,1)S(1)} %get-tuple-element.24), channel_id=1, source_target_pairs={{0,64},{64,128},{128,192},{192,256},{256,320},{320,384},{384,448},... | collective-permute-start | bytes 1572872 | tf_op jit(solution)/shard_map/ppermute | solution.py:188
  110.6 9.9 %psum.7 = f32[1,128]{1,0:T(1,128)S(1)} all-reduce(f32[1,128]{1,0:T(1,128)S(1)} %bitcast.22), channel_id=1, replica_groups=mesh['section'=12,'dp'=4,'tensor'=16] {'dp'}, use_global_device_ids=true, to_apply=%region_1.2 | all-reduce | flops 128 | bytes 1024 | tf_op jit(solution)/shard_map/psum | solution.py:189
  120.5 2.3 %collective-permute-done.15 = bf16[128,2048]{1,0:T(8,128)(2,1)S(1)} collective-permute-done((bf16[128,2048]{1,0:T(8,128)(2,1)S(1)}, bf16[128,2048]{1,0:T(8,128)(2,1)S(1)}, u32[]{:S(2)}, u32[]{:S(2)}) %collective-permute-start.15) | collective-permute-done | bytes 524320 | tf_op jit(solution)/shard_map/ppermute | solution.py:188
  122.9 0.9 fusion.1
  123.8 0.8 copy.9
  (11 shorter events, 0.2 us)
Async XLA Ops:
  0.6 110.0 %copy-start = (f32[1,8192]{1,0:T(1,128)S(1)}, f32[1,8192]{1,0:T(1,128)}, u32[]{:S(2)}) copy-start(f32[1,8192]{1,0:T(1,128)} %param.8) | copy-start | bytes 98308
  1.9 47.6 %copy-start.1 = (bf16[1,512,2048]{2,1,0:T(8,128)(2,1)S(1)}, bf16[1,512,2048]{2,1,0:T(8,128)(2,1)}, u32[]{:S(2)}) copy-start(bf16[1,512,2048]{2,1,0:T(8,128)(2,1)} %param.7) | copy-start | bytes 6291460
  1.9 10.1 %collective-permute-start = (bf16[2,128,512]{2,1,0:T(8,128)(2,1)S(1)}, bf16[2,128,512]{2,1,0:T(8,128)(2,1)S(1)}, u32[]{:S(2)}, u32[]{:S(2)}) collective-permute-start(bf16[2,128,512]{2,1,0:T(8,128)(2,1)S(1)} %pad_maximum_fusion.1), channel_id=1, source_target_pairs={{0,2},{1,3},{2,0},{3,1},{4,6},{5,7},{6,4},{7,5},{8,10},{9,11},{10,... | collective-permute-start | bytes 786440 | tf_op jit(solution)/shard_map/ppermute | solution.py:144
  12.0 48.6 %collective-permute-start.8 = (bf16[512,2048]{1,0:T(8,128)(2,1)}, bf16[512,2048]{1,0:T(8,128)(2,1)S(1)}, u32[]{:S(2)}, u32[]{:S(2)}) collective-permute-start(bf16[512,2048]{1,0:T(8,128)(2,1)} %bitcast.16), channel_id=1, source_target_pairs={{0,2},{1,3},{2,0},{3,1},{4,6},{5,7},{6,4},{7,5},{8,10},{9,11},{10,... | collective-permute-start | bytes 6291464 | tf_op jit(solution)/shard_map/ppermute | solution.py:149
  15.4 3.4 %collective-permute-start.1 = (bf16[2,128,512]{2,1,0:T(8,128)(2,1)S(1)}, bf16[2,128,512]{2,1,0:T(8,128)(2,1)S(1)}, u32[]{:S(2)}, u32[]{:S(2)}) collective-permute-start(bf16[2,128,512]{2,1,0:T(8,128)(2,1)S(1)} %pad_maximum_fusion.2), channel_id=1, source_target_pairs={{0,1},{1,0},{2,3},{3,2},{4,5},{5,4},{6,7},{7,6},{8,9},{9,8},{10,11... | collective-permute-start | bytes 786440 | tf_op jit(solution)/shard_map/ppermute | solution.py:146
  19.0 16.2 %collective-permute-start.2 = (bf16[4,64,512]{2,1,0:T(8,128)(2,1)S(1)}, bf16[4,64,512]{2,1,0:T(8,128)(2,1)S(1)}, u32[]{:S(2)}, u32[]{:S(2)}) collective-permute-start(bf16[4,64,512]{2,1,0:T(8,128)(2,1)S(1)} %get-tuple-element.28), channel_id=1, source_target_pairs={{0,16},{16,32},{32,48},{48,0},{1,17},{17,33},{33,49},{49,1},{2,18}... | collective-permute-start | bytes 786440 | tf_op jit(solution)/shard_map/ppermute | solution.py:152
  23.5 22.7 %collective-permute-start.5 = (bf16[4,64,512]{2,1,0:T(8,128)(2,1)S(1)}, bf16[4,64,512]{2,1,0:T(8,128)(2,1)S(1)}, u32[]{:S(2)}, u32[]{:S(2)}) collective-permute-start(bf16[4,64,512]{2,1,0:T(8,128)(2,1)S(1)} %get-tuple-element.27), channel_id=1, source_target_pairs={{0,48},{16,0},{32,16},{48,32},{1,49},{17,1},{33,17},{49,33},{2,50}... | collective-permute-start | bytes 786440 | tf_op jit(solution)/shard_map/ppermute | solution.py:153
  27.1 22.3 %collective-permute-start.3 = (bf16[4,64,512]{2,1,0:T(8,128)(2,1)S(1)}, bf16[4,64,512]{2,1,0:T(8,128)(2,1)S(1)}, u32[]{:S(2)}, u32[]{:S(2)}) collective-permute-start(bf16[4,64,512]{2,1,0:T(8,128)(2,1)S(1)} %get-tuple-element.27), channel_id=1, source_target_pairs={{0,16},{16,32},{32,48},{48,0},{1,17},{17,33},{33,49},{49,1},{2,18}... | collective-permute-start | bytes 786440 | tf_op jit(solution)/shard_map/ppermute | solution.py:155
  31.2 22.3 %collective-permute-start.4 = (bf16[4,64,512]{2,1,0:T(8,128)(2,1)S(1)}, bf16[4,64,512]{2,1,0:T(8,128)(2,1)S(1)}, u32[]{:S(2)}, u32[]{:S(2)}) collective-permute-start(bf16[4,64,512]{2,1,0:T(8,128)(2,1)S(1)} %get-tuple-element.28), channel_id=1, source_target_pairs={{0,48},{16,0},{32,16},{48,32},{1,49},{17,1},{33,17},{49,33},{2,50}... | collective-permute-start | bytes 786440 | tf_op jit(solution)/shard_map/ppermute | solution.py:154
  35.2 19.7 %collective-permute-start.6 = (bf16[4,64,512]{2,1,0:T(8,128)(2,1)S(1)}, bf16[4,64,512]{2,1,0:T(8,128)(2,1)S(1)}, u32[]{:S(2)}, u32[]{:S(2)}) collective-permute-start(bf16[4,64,512]{2,1,0:T(8,128)(2,1)S(1)} %collective-permute-done.2.refs_1_), channel_id=1, source_target_pairs={{0,16},{16,32},{32,48},{48,0},{1,17},{17,33},{33,49},{49,1},{2,18}... | collective-permute-start | bytes 786440 | tf_op jit(solution)/shard_map/ppermute | solution.py:156
  46.2 13.3 %collective-permute-start.7 = (bf16[4,64,512]{2,1,0:T(8,128)(2,1)S(1)}, bf16[4,64,512]{2,1,0:T(8,128)(2,1)S(1)}, u32[]{:S(2)}, u32[]{:S(2)}) collective-permute-start(bf16[4,64,512]{2,1,0:T(8,128)(2,1)S(1)} %collective-permute-done.5.refs_4_), channel_id=1, source_target_pairs={{0,48},{16,0},{32,16},{48,32},{1,49},{17,1},{33,17},{49,33},{2,50}... | collective-permute-start | bytes 786440 | tf_op jit(solution)/shard_map/ppermute | solution.py:157
  49.4 13.1 %collective-permute-start.10 = (bf16[512,2048]{1,0:T(8,128)(2,1)S(1)}, bf16[512,2048]{1,0:T(8,128)(2,1)S(1)}, u32[]{:S(2)}, u32[]{:S(2)}) collective-permute-start(bf16[512,2048]{1,0:T(8,128)(2,1)S(1)} %bitcast.17), channel_id=1, source_target_pairs={{0,1},{1,0},{2,3},{3,2},{4,5},{5,4},{6,7},{7,6},{8,9},{9,8},{10,11... | collective-permute-start | bytes 6291464 | tf_op jit(solution)/shard_map/ppermute | solution.py:160
  60.6 7.1 %collective-permute-start.9 = (bf16[512,2048]{1,0:T(8,128)(2,1)S(1)}, bf16[512,2048]{1,0:T(8,128)(2,1)S(1)}, u32[]{:S(2)}, u32[]{:S(2)}) collective-permute-start(bf16[512,2048]{1,0:T(8,128)(2,1)S(1)} %collective-permute-done.8.refs_7_), channel_id=1, source_target_pairs={{0,1},{1,0},{2,3},{3,2},{4,5},{5,4},{6,7},{7,6},{8,9},{9,8},{10,11... | collective-permute-start | bytes 6291464 | tf_op jit(solution)/shard_map/ppermute | solution.py:161
  71.3 20.7 %collective-permute-start.11 = (bf16[2,128,1024]{2,1,0:T(8,128)(2,1)S(1)}, bf16[2,128,1024]{2,1,0:T(8,128)(2,1)S(1)}, u32[]{:S(2)}, u32[]{:S(2)}) collective-permute-start(bf16[2,128,1024]{2,1,0:T(8,128)(2,1)S(1)} %get-tuple-element.16), channel_id=1, source_target_pairs={{0,8},{1,9},{2,10},{3,11},{4,12},{5,13},{6,14},{7,15},{8,0},{9,1},... | collective-permute-start | bytes 1572872 | tf_op jit(solution)/shard_map/ppermute | solution.py:169
  79.5 17.5 %collective-permute-start.13 = (bf16[2,128,1024]{2,1,0:T(8,128)(2,1)S(1)}, bf16[2,128,1024]{2,1,0:T(8,128)(2,1)S(1)}, u32[]{:S(2)}, u32[]{:S(2)}) collective-permute-start(bf16[2,128,1024]{2,1,0:T(8,128)(2,1)S(1)} %get-tuple-element.20), channel_id=1, source_target_pairs={{0,6},{1,7},{2,4},{3,5},{4,2},{5,3},{6,0},{7,1},{8,14},{9,15},{10,... | collective-permute-start | bytes 1572872 | tf_op jit(solution)/shard_map/ppermute | solution.py:168
  92.1 14.8 %copy-start.2 = (bf16[1,128,2048]{2,1,0:T(8,128)(2,1)S(1)}, bf16[1,128,2048]{2,1,0:T(8,128)(2,1)}, u32[]{:S(2)}) copy-start(bf16[1,128,2048]{2,1,0:T(8,128)(2,1)} %param.6) | copy-start | bytes 1572868
  92.2 11.4 %collective-permute-start.12 = (bf16[128,1024]{1,0:T(8,128)(2,1)S(1)}, bf16[128,1024]{1,0:T(8,128)(2,1)S(1)}, u32[]{:S(2)}, u32[]{:S(2)}) collective-permute-start(bf16[128,1024]{1,0:T(8,128)(2,1)S(1)} %get-tuple-element.18), channel_id=1, source_target_pairs={{0,6},{1,7},{2,4},{3,5},{4,2},{5,3},{6,0},{7,1},{8,14},{9,15},{10,... | collective-permute-start | bytes 786440 | tf_op jit(solution)/shard_map/ppermute | solution.py:172
  97.1 9.7 %collective-permute-start.14 = (bf16[128,1024]{1,0:T(8,128)(2,1)S(1)}, bf16[128,1024]{1,0:T(8,128)(2,1)S(1)}, u32[]{:S(2)}, u32[]{:S(2)}) collective-permute-start(bf16[128,1024]{1,0:T(8,128)(2,1)S(1)} %get-tuple-element.22), channel_id=1, source_target_pairs={{0,8},{1,9},{2,10},{3,11},{4,12},{5,13},{6,14},{7,15},{8,0},{9,1},... | collective-permute-start | bytes 786440 | tf_op jit(solution)/shard_map/ppermute | solution.py:173
  107.2 15.7 %collective-permute-start.15 = (bf16[128,2048]{1,0:T(8,128)(2,1)S(1)}, bf16[128,2048]{1,0:T(8,128)(2,1)S(1)}, u32[]{:S(2)}, u32[]{:S(2)}) collective-permute-start(bf16[128,2048]{1,0:T(8,128)(2,1)S(1)} %get-tuple-element.24), channel_id=1, source_target_pairs={{0,64},{64,128},{128,192},{192,256},{256,320},{320,384},{384,448},... | collective-permute-start | bytes 1572872 | tf_op jit(solution)/shard_map/ppermute | solution.py:188
